TPU v7x, 32 devices: a whole 2x2x4 slice. The times are simulated.
32 devices in a mesh: parts: 2 (over y), blk: 4 (over z), ao: 2 (over x), sub: 2 (over core).
Axes of the slice: x: 2, y: 2, z: 4, core: 2. Of those that a mesh axis runs over, the one named last changes fastest.
Arguments:
- coulomb_three: bfloat16 [1024, 256, 512], P(('parts', 'ao'), ('blk', 'sub')), parts along dimension 0, may hold values from -0.23925781 to 0.23925781
- three_mask: int32 [64, 16, 32], P(('parts', 'ao'), ('blk', 'sub')), parts along dimension 0, may hold values 0 or 1
- g_occ: bfloat16 [1024, 512], P(('parts', 'blk', 'sub')), parts along dimension 0, may hold values from -8 to 8
- g_virt: bfloat16 [1024, 512], P(('parts', 'blk', 'sub')), parts along dimension 0, may hold values from -8 to 8
- occ_mask: int32 [64, 32], P('parts'), parts along dimension 0, may hold values from 0 to 1, as said below
- virt_mask: int32 [64, 32], P('parts'), parts along dimension 0, may hold values from 0 to 1, as said below
Outputs:
- chi_band: float32 [512, 3, 32], P(('parts', 'blk', 'sub')), parts along dimension 0
There are 2 independent parts, one for each index of `parts`. A program takes and returns all parts, laid end to end along the dimension named above; each array names one. Nothing has to cross between parts.
Inputs may be any that keep to these rules, and one draw needn't show every extreme that they name: `occ_mask`: symmetric; every diagonal block is 1. `virt_mask`: symmetric; every diagonal block is 1.
All inputs are finite; a program needn't handle non-finite values. No bound on the sum of `three_mask` on one device may be relied on, other than what follows from the above.
Results may differ from a plain program's by a relative error of at most 0.0003.
Values may be sent and summed in bfloat16 or wider, within the bound.
A program may use at most 256 MiB of HBM per device.

v0:
```python
import jax
import jax.numpy as jnp
from jax import lax
from jax.sharding import PartitionSpec as P

NAO = 512
BS = 16
ABLK = 16
REACH = 1


def from_behind(x, axis, by):
    count = lax.axis_size(axis)
    pairs = [(i, i + by) for i in range(count) if 0 <= i + by < count]
    return lax.ppermute(x, axis, pairs)


def mask_green(green, blocks):
    nblocks = blocks.shape[0]
    shaped = green.reshape(nblocks, BS, nblocks, BS)
    return (shaped * blocks[:, None, :, None].astype(green.dtype)).reshape(green.shape)


def mask_three(three_blk, mask_blk):
    nu_blocks = mask_blk.shape[0]
    aux_blocks = mask_blk.shape[1]
    mu_blocks = mask_blk.shape[2]
    shaped = three_blk.reshape(nu_blocks, BS, aux_blocks, ABLK, mu_blocks, BS)
    weights = mask_blk[:, None, :, None, :, None].astype(three_blk.dtype)
    return (shaped * weights).reshape(three_blk.shape)


def aux_major(tensor):
    return jnp.transpose(tensor, (1, 0, 2)).reshape(
        tensor.shape[1], tensor.shape[0] * tensor.shape[2]
    )


def contract(factor, tensor):
    return lax.dot_general(
        factor, tensor, (((1,), (1,)), ((), ())), preferred_element_type=jnp.float32
    )


def neighbours(source):
    fetched = {}
    for direction in (1, -1):
        fetched[direction] = from_behind(source, ("blk", "sub"), -direction * 1)
    return fetched


def body(coulomb_three, three_mask, g_occ, g_virt, occ_mask, virt_mask):
    slab_width = coulomb_three.shape[0]
    aux_local = coulomb_three.shape[1]
    three_eff = mask_three(coulomb_three, three_mask)
    occ_full, virt_full = (
        lax.all_gather(g_occ, ("blk", "sub"), axis=0, tiled=True),
        lax.all_gather(g_virt, ("blk", "sub"), axis=0, tiled=True),
    )
    occ_eff = mask_green(occ_full, occ_mask)
    virt_eff = mask_green(virt_full, virt_mask)
    left = jnp.dot(
        three_eff.reshape(slab_width * aux_local, NAO), occ_eff, preferred_element_type=jnp.float32
    )
    left = left.astype(jnp.bfloat16).reshape(slab_width, aux_local, NAO)
    summed = lax.dot_general(
        virt_eff,
        lax.all_to_all(left, "ao", split_axis=2, concat_axis=0, tiled=True),
        (((0,), (0,)), ((), ())),
        preferred_element_type=jnp.float32,
    )
    rounded = summed.astype(jnp.bfloat16)
    right = lax.all_to_all(rounded, "ao", split_axis=0, concat_axis=2, tiled=True)
    right_flat = aux_major(right)
    three_flat = aux_major(three_eff)
    band_tiles = {0: contract(right_flat, three_flat)}
    fetched = neighbours(right_flat)
    for offset in fetched:
        computed = contract(fetched[offset], three_flat)
        band_tiles[-offset] = from_behind(computed, ("blk", "sub"), offset)
    ordered = [band_tiles[offset] for offset in range(-REACH, REACH + 1)]
    combined = jnp.stack(ordered, axis=1)
    return lax.psum(combined, "ao")


def solution(mesh):
    placed = (
        P(("parts", "ao"), ("blk", "sub"), None),
        P(("parts", "ao"), ("blk", "sub"), None),
        P(("parts", "blk", "sub"), None),
        P(("parts", "blk", "sub"), None),
        P("parts", None),
        P("parts", None),
    )
    return jax.shard_map(
        body,
        mesh=mesh,
        in_specs=placed,
        out_specs=P(("parts", "blk", "sub"), None, None),
        check_vma=False,
    )
```

profile of v0, /device:TPU:8, one launch (start us, length us, event | category | flops | bytes accessed | tf_op | source)
XLA Modules:
  0.0 618.2 jit_solution(1004467555262368278)
XLA Ops:
  0.0 0.7 convert_element_type.19
  1.4 15.2 %all_gather.7 = bf16[512,512]{1,0:T(8,128)(2,1)S(1)} all-gather(bf16[64,512]{1,0:T(8,128)(2,1)} %param.8), channel_id=1, replica_groups=mesh['parts'=2,'blk'=4,'ao'=2,'sub'=2] {'blk','sub'}, dimensions={0}, use_global_device_ids=true | all-gather | bytes 589824 | tf_op jit(solution)/shard_map/all_gather | solution.py:57
  16.7 2.6 mul.44
  19.2 7.8 %mul.45 = bf16[512,512]{1,0:T(8,128)(2,1)S(1)} reshape(bf16[32,16,32,16]{3,2,1,0:T(8,128)(2,1)} %mul.44) | data formatting | bytes 1048576 | tf_op jit(solution)/shard_map/mul | solution.py:21
  27.0 21.3 %mul.41 = bf16[16,16,2,16,32,16]{5,4,3,2,1,0:T(8,128)(2,1)} broadcast(bf16[16,2,32]{2,1,0:T(2,128)(2,1)S(1)} %convert_element_type.19), dimensions={0,2,4} | broadcast | bytes 8390656 | tf_op jit(solution)/shard_map/mul | solution.py:30
  48.3 109.2 %mul.42 = bf16[8192,512]{1,0:T(8,128)(2,1)} reshape(bf16[16,16,2,16,32,16]{5,4,3,2,1,0:T(8,128)(2,1)} %mul.41) | data formatting | bytes 16777216 | tf_op jit(solution)/shard_map/mul | solution.py:30
  157.5 6.4 %bitcast_multiply_fusion = bf16[8192,512]{1,0:T(8,128)(2,1)S(1)} fusion(bf16[8192,512]{1,0:T(8,128)(2,1)} %mul.42, bf16[256,32,512]{2,1,0:T(8,128)(2,1)} %param.6), kind=kLoop, calls=%fused_computation.4 | loop fusion | flops 4194304 | bytes 25165824 | tf_op jit(solution)/shard_map/mul | solution.py:30
  163.9 6.7 %convolution_convert_fusion = bf16[8192,512]{1,0:T(8,128)(2,1)} fusion(bf16[8192,512]{1,0:T(8,128)(2,1)S(1)} %bitcast_multiply_fusion, bf16[512,512]{1,0:T(8,128)(2,1)S(1)} %all_gather.7, bf16[512,512]{1,0:T(8,128)(2,1)S(1)} %mul.45), kind=kOutput, calls=%fused_computation | convolution fusion | flops 4299423744 | bytes 17825792 | tf_op jit(solution)/shard_map/dot_general | solution.py:62
  170.6 15.9 %copy.22 = bf16[256,32,512]{0,1,2:T(8,128)(2,1)} copy(bf16[256,32,512]{2,1,0:T(8,128)(2,1)} %bitcast.57) | data formatting | bytes 16777216 | tf_op jit(solution)/shard_map/reshape | solution.py:65
  186.5 7.1 %all-to-all-start = ((bf16[256,32,512]{0,1,2:T(8,128)(2,1)}), bf16[256,32,512]{0,1,2:T(8,128)(2,1)}, u32[]{:S(2)}, u32[]{:S(2)}) async-start(bf16[256,32,512]{0,1,2:T(8,128)(2,1)} %copy.22), calls=%async_computation | async-start | bytes 16777216 | tf_op jit(solution)/shard_map/all_to_all | solution.py:68
  193.7 2.6 mul.38
  196.3 7.8 %mul.39 = bf16[512,512]{1,0:T(8,128)(2,1)S(1)} reshape(bf16[32,16,32,16]{3,2,1,0:T(8,128)(2,1)} %mul.38) | data formatting | bytes 1048576 | tf_op jit(solution)/shard_map/mul | solution.py:21
  204.1 15.3 %all_gather.6 = bf16[512,512]{1,0:T(8,128)(2,1)S(1)} all-gather(bf16[64,512]{1,0:T(8,128)(2,1)S(1)} %copy-done), channel_id=1, replica_groups=mesh['parts'=2,'blk'=4,'ao'=2,'sub'=2] {'blk','sub'}, dimensions={0}, use_global_device_ids=true | all-gather | bytes 589824 | tf_op jit(solution)/shard_map/all_gather | solution.py:58
  219.4 67.4 %all-to-all-done = bf16[256,32,512]{0,1,2:T(8,128)(2,1)} async-done(((bf16[256,32,512]{0,1,2:T(8,128)(2,1)}), bf16[256,32,512]{0,1,2:T(8,128)(2,1)}, u32[]{:S(2)}, u32[]{:S(2)}) %all-to-all-start) | async-done | bytes 8388640 | tf_op jit(solution)/shard_map/all_to_all | solution.py:68
  286.8 13.8 %copy.23 = bf16[256,32,2,256]{3,0,2,1:T(8,128)(2,1)} copy(bf16[256,32,2,256]{0,1,3,2:T(8,128)(2,1)} %bitcast.3) | data formatting | bytes 16777216 | tf_op jit(solution)/shard_map/all_to_all | solution.py:68
  300.5 10.1 %convolution_convert_fusion.1 = bf16[512,32,256]{2,0,1:T(8,128)(2,1)} fusion(bf16[512,32,256]{2,0,1:T(8,128)(2,1)} %bitcast.58, bf16[512,512]{1,0:T(8,128)(2,1)S(1)} %all_gather.6, bf16[512,512]{1,0:T(8,128)(2,1)S(1)} %mul.39), kind=kOutput, calls=%fused_computation.6 | convolution fusion | flops 4300210176 | bytes 17825792 | tf_op jit(solution)/shard_map/dot_general | solution.py:66
  310.6 11.5 %copy.25 = bf16[512,32,256]{2,1,0:T(8,128)(2,1)} copy(bf16[512,32,256]{2,0,1:T(8,128)(2,1)} %convolution_convert_fusion.1) | data formatting | bytes 16777216 | tf_op jit(solution)/shard_map/convert_element_type | solution.py:72
  322.1 96.9 %all_to_all.36 = bf16[512,32,256]{2,1,0:T(8,128)(2,1)S(1)} all-to-all(bf16[512,32,256]{2,1,0:T(8,128)(2,1)} %copy.25), channel_id=1, replica_groups=mesh['parts'=2,'blk'=4,'ao'=2,'sub'=2] {'ao'}, dimensions={0} | all-to-all | bytes 16777216 | tf_op jit(solution)/shard_map/all_to_all | solution.py:73
  419.0 8.2 %copy.34 = bf16[2,256,32,256]{3,0,2,1:T(2,128)(2,1)} copy(bf16[2,256,32,256]{3,2,1,0:T(8,128)(2,1)S(1)} %bitcast.53) | data formatting | bytes 16777216 | tf_op jit(solution)/shard_map/all_to_all | solution.py:73
  427.2 14.1 %all_to_all.33 = bf16[256,32,512]{2,1,0:T(8,128)(2,1)} reshape(bf16[256,32,2,256]{3,2,1,0:T(2,128)(2,1)} %bitcast.54) | data formatting | bytes 16777216 | tf_op jit(solution)/shard_map/all_to_all | solution.py:73
  441.3 7.4 %copy.31 = bf16[256,4,8,512]{3,2,0,1:T(8,128)(2,1)} copy(bf16[256,4,8,512]{3,2,1,0:T(8,128)(2,1)} %bitcast.52) | data formatting | bytes 16777216 | tf_op jit(solution)/shard_map/reshape | solution.py:34
  448.7 1.9 collective-permute-start.2
  450.6 3.9 collective-permute-start
  454.5 109.2 %mul.47 = bf16[256,32,512]{2,1,0:T(8,128)(2,1)} reshape(bf16[16,16,2,16,32,16]{5,4,3,2,1,0:T(8,128)(2,1)} %mul.41) | data formatting | bytes 16777216 | tf_op jit(solution)/shard_map/mul | solution.py:30
  563.7 8.9 %multiply_bitcast_fusion = bf16[256,4,8,512]{3,2,1,0:T(8,128)(2,1)} fusion(bf16[256,32,512]{2,1,0:T(8,128)(2,1)} %param.6, bf16[256,32,512]{2,1,0:T(8,128)(2,1)} %mul.47), kind=kLoop, calls=%fused_computation.7 | loop fusion | flops 4194304 | bytes 25165824
  572.6 7.4 %copy.32 = bf16[256,4,8,512]{3,2,0,1:T(8,128)(2,1)} copy(bf16[256,4,8,512]{3,2,1,0:T(8,128)(2,1)} %multiply_bitcast_fusion) | data formatting | bytes 16777216 | tf_op jit(solution)/shard_map/reshape | solution.py:34
  580.0 8.2 %fusion.13 = f32[32,32]{1,0:T(8,128)S(1)} fusion(bf16[32,131072]{1,0:T(8,128)(2,1)} %collective-permute-done.2, bf16[32,131072]{1,0:T(8,128)(2,1)} %bitcast.50), kind=kOutput, calls=%fused_computation.15 | convolution fusion | flops 268435456 | bytes 16781312 | tf_op jit(solution)/shard_map/dot_general | solution.py:40
  588.3 3.8 collective-permute-start.3
  592.0 8.1 %fusion.12 = f32[32,32]{1,0:T(8,128)S(1)} fusion(bf16[32,131072]{1,0:T(8,128)(2,1)} %collective-permute-done, bf16[32,131072]{1,0:T(8,128)(2,1)} %bitcast.51), kind=kOutput, calls=%fused_computation.14 | convolution fusion | flops 268435456 | bytes 16781312 | tf_op jit(solution)/shard_map/dot_general | solution.py:40
  600.1 1.9 collective-permute-start.1
  602.1 8.1 %fusion.4 = f32[32,1,32]{2,0,1:T(8,128)S(1)} fusion(bf16[256,32,512]{2,1,0:T(8,128)(2,1)S(1)} %bitcast.49, bf16[256,32,512]{2,1,0:T(8,128)(2,1)} %mul.47, bf16[256,32,512]{2,1,0:T(8,128)(2,1)} %all_to_all.33), kind=kOutput, calls=%fused_computation.9 | convolution fusion | flops 272629760 | bytes 25169920 | tf_op jit(solution)/shard_map/dot_general | solution.py:40
  610.2 8.0 %psum.7 = f32[32,3,32]{2,0,1:T(8,128)} all-reduce(f32[32,3,32]{2,0,1:T(8,128)S(1)} %pad_maximum_fusion), channel_id=1, replica_groups=mesh['parts'=2,'blk'=4,'ao'=2,'sub'=2] {'ao'}, use_global_device_ids=true, to_apply=%region_0.0 | all-reduce | flops 3072 | bytes 24576 | tf_op jit(solution)/shard_map/psum | solution.py:83
  (16 shorter events, 0.8 us)
Async XLA Ops:
  186.5 7.1 %copy-start.1 = (s32[32,32]{1,0:T(8,128)S(1)}, s32[32,32]{1,0:T(8,128)}, u32[]{:S(2)}) copy-start(s32[32,32]{1,0:T(8,128)} %param.11) | copy-start | bytes 12292
  186.5 100.2 %all-to-all-start = ((bf16[256,32,512]{0,1,2:T(8,128)(2,1)}), bf16[256,32,512]{0,1,2:T(8,128)(2,1)}, u32[]{:S(2)}, u32[]{:S(2)}) async-start(bf16[256,32,512]{0,1,2:T(8,128)(2,1)} %copy.22), calls=%async_computation | async-start | bytes 16777216 | tf_op jit(solution)/shard_map/all_to_all | solution.py:68
  193.6 10.4 %copy-start = (bf16[64,512]{1,0:T(8,128)(2,1)S(1)}, bf16[64,512]{1,0:T(8,128)(2,1)}, u32[]{:S(2)}) copy-start(bf16[64,512]{1,0:T(8,128)(2,1)} %param.9) | copy-start | bytes 196612
  448.7 131.3 %collective-permute-start.2 = (bf16[32,131072]{1,0:T(8,128)(2,1)}, bf16[32,131072]{1,0:T(8,128)(2,1)}, u32[]{:S(2)}, u32[]{:S(2)}) collective-permute-start(bf16[32,131072]{1,0:T(8,128)(2,1)} %bitcast.55), channel_id=1, source_target_pairs={{0,1},{1,4},{4,5},{5,8},{8,9},{9,12},{12,13},{2,3},{3,6},{6,7},{7,... | collective-permute-start | bytes 25165832 | tf_op jit(solution)/shard_map/ppermute | solution.py:15
  450.6 141.4 %collective-permute-start = (bf16[32,131072]{1,0:T(8,128)(2,1)}, bf16[32,131072]{1,0:T(8,128)(2,1)}, u32[]{:S(2)}, u32[]{:S(2)}) collective-permute-start(bf16[32,131072]{1,0:T(8,128)(2,1)} %bitcast.56), channel_id=1, source_target_pairs={{1,0},{4,1},{5,4},{8,5},{9,8},{12,9},{13,12},{3,2},{6,3},{7,6},{10... | collective-permute-start | bytes 25165832 | tf_op jit(solution)/shard_map/ppermute | solution.py:15
  580.0 22.0 %slice-start = ((s8[8388608]{0:T(1024)(128)(4,1)}), s8[4194304]{0:T(1024)(128)(4,1)S(1)}, s32[]{:S(2)}) async-start(s8[8388608]{0:T(1024)(128)(4,1)} %bitcast.48), calls=%async_computation.2 | async-start | bytes 8388608
  588.2 13.8 %slice-start.1 = ((s8[8388608]{0:T(1024)(128)(4,1)}), s8[4194304]{0:T(1024)(128)(4,1)S(1)}, s32[]{:S(2)}) async-start(s8[8388608]{0:T(1024)(128)(4,1)} %bitcast.48), calls=%async_computation.3 | async-start | bytes 8388608
  588.3 21.9 %collective-permute-start.3 = (f32[32,32]{1,0:T(8,128)S(1)}, f32[32,32]{1,0:T(8,128)S(1)}, u32[]{:S(2)}, u32[]{:S(2)}) collective-permute-start(f32[32,32]{1,0:T(8,128)S(1)} %fusion.13), channel_id=1, source_target_pairs={{1,0},{4,1},{5,4},{8,5},{9,8},{12,9},{13,12},{3,2},{6,3},{7,6},{10... | collective-permute-start | bytes 12296 | tf_op jit(solution)/shard_map/ppermute | solution.py:15
  600.1 10.0 %collective-permute-start.1 = (f32[32,32]{1,0:T(8,128)S(1)}, f32[32,32]{1,0:T(8,128)S(1)}, u32[]{:S(2)}, u32[]{:S(2)}) collective-permute-start(f32[32,32]{1,0:T(8,128)S(1)} %fusion.12), channel_id=1, source_target_pairs={{0,1},{1,4},{4,5},{5,8},{8,9},{9,12},{12,13},{2,3},{3,6},{6,7},{7,... | collective-permute-start | bytes 12296 | tf_op jit(solution)/shard_map/ppermute | solution.py:15
where the time goes:
time: 621 us; the launch traced here: 618 us
  local copies, waits for them, and re-layouts  339 us (55%)
  blocking collectives  135 us (22%)
  waiting for transfers between devices  67.4 us (11%)
  matrix products  41.1 us (7%)
  starting transfers between devices  18.6 us (3%)
  other arithmetic  16.7 us (3%)
    mul x3, local copies, waits for them, and re-layouts, mask_three(): return (shaped * weights).reshape(three_blk.shape)  240 us
    all_to_all x1, blocking collectives, body(): lax.all_to_all(rounded, 'ao', split_axis=0, concat_axis=2, tiled=True)  96.9 us
    all_to_all x1, waiting for transfers between devices, body(): lax.all_to_all(left, 'ao', split_axis=2, concat_axis=0, tiled=True)  67.4 us
    dot_general x3, matrix products, contract(): lax.dot_general(factor, tensor, (((1,), (1,)), ((), ())), preferred_eleme...  24.3 us
    all_to_all x2, local copies, waits for them, and re-layouts, body(): lax.all_to_all(rounded, 'ao', split_axis=0, concat_axis=2, tiled=True)  22.3 us
    mul x4, local copies, waits for them, and re-layouts, mask_green(): shaped * blocks[:, None, :, None].astype(green.dtype)  20.7 us
    reshape x1, local copies, waits for them, and re-layouts, body(): left = left.astype(jnp.bfloat16).reshape(slab_width, aux_local, NAO)  15.9 us
    all_gather x1, blocking collectives, body(): lax.all_gather(g_virt, ('blk', 'sub'), axis=0, tiled=True)  15.3 us
  transfers between devices with their start and end apart: 5, of which 1 were waited for; matrix products, arithmetic and copies ran while one was open for 26% of the time, Pallas kernels for 0%

commit v1 on v0

v1 whole, which is shorter than its diff:
```python
import jax
import jax.numpy as jnp
from jax import lax
from jax.experimental import pallas as pl
from jax.experimental.pallas import tpu as pltpu
from jax.sharding import PartitionSpec as P

BS = 16
ABLK = 16
CHUNK = 128
VMEM_LIMIT = 48 * 1024 * 1024


def shift(x, axis, by):
    count = lax.axis_size(axis)
    pairs = [(i, i + by) for i in range(count) if 0 <= i + by < count]
    return lax.ppermute(x, axis, pairs)


def spread(blocks, size):
    row = lax.broadcasted_iota(jnp.int32, (blocks, size), 0)
    col = lax.broadcasted_iota(jnp.int32, (blocks, size), 1)
    return (row == col // BS).astype(jnp.bfloat16)


def widen_last(mask, size):
    count = mask.shape[-1]
    flat = mask.astype(jnp.bfloat16).reshape(-1, count)
    wide = jnp.dot(flat, spread(count, size), preferred_element_type=jnp.float32)
    return wide.astype(jnp.bfloat16).reshape(mask.shape[:-1] + (size,))


def mask_green(green, blocks):
    count = blocks.shape[0]
    wide = widen_last(blocks, green.shape[1])
    shaped = green.reshape(count, green.shape[0] // count, green.shape[1])
    return (shaped * wide[:, None, :]).reshape(green.shape)


def mask_three(three, mask):
    wide = widen_last(mask, three.shape[2])
    shaped = three.reshape(mask.shape[0], BS, mask.shape[1], ABLK, three.shape[2])
    return (shaped * wide[:, None, :, None, :]).reshape(three.shape)


def transform_kernel(own_ref, oth_ref, occ_ref, virt_ref, send_ref, keep_ref, left_ref, right_ref):
    half, share, depth = own_ref.shape
    width = occ_ref.shape[1]
    full = 2 * half
    step = 64
    occ = occ_ref[...]
    for which, ref in enumerate((own_ref, oth_ref)):

        @pl.loop(0, half // step)
        def _(i, ref=ref, which=which):
            rows = ref[pl.ds(i * step, step)].reshape(step * share, depth)
            at = pl.multiple_of((which * half + i * step) * share, step * share)
            left_ref[pl.ds(at, step * share), :] = jnp.dot(
                rows, occ, preferred_element_type=jnp.float32
            )

    for p in range(0, share, 2):
        pair = [left_ref[pl.ds(p + k, full, stride=share), :].astype(jnp.bfloat16) for k in (0, 1)]
        out = lax.dot_general(
            virt_ref[...],
            jnp.concatenate(pair, axis=1),
            (((0,), (0,)), ((), ())),
            preferred_element_type=jnp.float32,
        )
        for k in (0, 1):
            right_ref[pl.ds(p + k, full, stride=share), :] = out[:, k * width : (k + 1) * width]
    for which, ref in enumerate((send_ref, keep_ref)):

        @pl.loop(0, half // step)
        def _(i, ref=ref, which=which):
            at = pl.multiple_of((which * half + i * step) * share, step * share)
            rows = right_ref[pl.ds(at, step * share), :].astype(jnp.bfloat16)
            ref[pl.ds(i * step, step)] = rows.reshape(step, share, width)


def transform(own, oth, occ, virt):
    half, share, depth = own.shape
    width = occ.shape[1]
    out = jax.ShapeDtypeStruct((half, share, width), jnp.bfloat16)
    vmem = pl.BlockSpec(memory_space=pltpu.VMEM)
    return pl.pallas_call(
        transform_kernel,
        out_shape=(out, out),
        in_specs=[vmem] * 4,
        out_specs=(vmem, vmem),
        scratch_shapes=[pltpu.VMEM((2 * half * share, width), jnp.float32)] * 2,
        compiler_params=pltpu.CompilerParams(vmem_limit_bytes=VMEM_LIMIT),
        cost_estimate=pl.CostEstimate(
            flops=4 * half * share * width * (depth + 2 * half) * 2,
            bytes_accessed=4 * half * share * depth + 4 * half * share * width,
            transcendentals=0,
        ),
        name="transform",
    )(own, oth, occ, virt)


def band_kernel(right_ref, before_ref, here_ref, after_ref, out_ref):
    count, share, width = right_ref.shape

    @pl.when(pl.program_id(0) == 0)
    def _():
        out_ref[...] = jnp.zeros_like(out_ref)

    total = jnp.zeros(out_ref.shape, jnp.float32)
    for s in range(0, count, 2):
        rights = jnp.concatenate([right_ref[s], right_ref[s + 1]], axis=1)
        threes = jnp.concatenate(
            [
                jnp.concatenate([ref[s], ref[s + 1]], axis=1)
                for ref in (before_ref, here_ref, after_ref)
            ],
            axis=0,
        )
        total += lax.dot_general(
            rights, threes, (((1,), (1,)), ((), ())), preferred_element_type=jnp.float32
        )
    out_ref[...] += total


def band(right, threes, chunk):
    half, share, width = right.shape
    aux = threes[0].shape[1]
    rows = 32
    block = pl.BlockSpec((rows, aux, width), lambda i: (i, 0, chunk))
    return pl.pallas_call(
        band_kernel,
        grid=(half // rows,),
        out_shape=jax.ShapeDtypeStruct((share, 3 * aux), jnp.float32),
        in_specs=[pl.BlockSpec((rows, share, width), lambda i: (i, 0, 0))] + [block] * 3,
        out_specs=pl.BlockSpec((share, 3 * aux), lambda i: (0, 0)),
        compiler_params=pltpu.CompilerParams(vmem_limit_bytes=VMEM_LIMIT),
        cost_estimate=pl.CostEstimate(
            flops=2 * half * share * 3 * aux * width * 8,
            bytes_accessed=2 * half * width * (share + 3 * aux),
            transcendentals=0,
        ),
        name="band",
    )(right, *threes)


def body_pair(three, three_mask, g_occ, g_virt, occ_mask, virt_mask):
    half, aux, depth = three.shape
    share = aux // 2
    me = lax.axis_index("ao")
    swap = [(0, 1), (1, 0)]
    eff = mask_three(three, three_mask)
    low, high = eff[:, :share], eff[:, share:]
    first = me == 0
    own = jnp.where(first, low, high)
    oth = lax.ppermute(jnp.where(first, high, low), "ao", swap)
    both = lax.all_gather(jnp.stack([g_occ, g_virt]), ("blk", "sub"), axis=1, tiled=True)
    occ = mask_green(both[0], occ_mask)
    virt = mask_green(both[1], virt_mask)
    rows = jnp.where(first, virt, jnp.concatenate([virt[half:], virt[:half]], axis=0))
    virt = jnp.where(first, jnp.concatenate([rows[:, half:], rows[:, :half]], axis=1), rows)
    threes = (shift(eff, ("blk", "sub"), 1), eff, shift(eff, ("blk", "sub"), -1))
    kept, got = 0.0, 0.0
    for c in range(depth // CHUNK):
        send, keep = transform(own, oth, occ[:, c * CHUNK : (c + 1) * CHUNK], virt)
        recv = lax.ppermute(send, "ao", swap)
        kept = kept + band(keep, threes, c)
        got = got + band(recv, threes, c)
    chi = jnp.where(
        first, jnp.concatenate([kept, got], axis=0), jnp.concatenate([got, kept], axis=0)
    )
    return lax.psum(chi, "ao").reshape(aux, 3, aux)


def body_any(three, three_mask, g_occ, g_virt, occ_mask, virt_mask):
    eff = mask_three(three, three_mask)
    occ = mask_green(lax.all_gather(g_occ, ("blk", "sub"), axis=0, tiled=True), occ_mask)
    virt = mask_green(lax.all_gather(g_virt, ("blk", "sub"), axis=0, tiled=True), virt_mask)
    whole = lax.all_to_all(eff, "ao", split_axis=1, concat_axis=0, tiled=True)
    left = lax.dot_general(
        whole, occ, (((2,), (0,)), ((), ())), preferred_element_type=jnp.float32
    ).astype(jnp.bfloat16)
    right = lax.dot_general(
        virt, left, (((0,), (0,)), ((), ())), preferred_element_type=jnp.float32
    ).astype(jnp.bfloat16)
    right = lax.all_to_all(right, "ao", split_axis=0, concat_axis=1, tiled=True)
    tiles = [
        lax.dot_general(
            right, other, (((0, 2), (0, 2)), ((), ())), preferred_element_type=jnp.float32
        )
        for other in (shift(eff, ("blk", "sub"), 1), eff, shift(eff, ("blk", "sub"), -1))
    ]
    return lax.psum(jnp.stack(tiles, axis=1), "ao")


def solution(mesh):
    placed = (
        P(("parts", "ao"), ("blk", "sub"), None),
        P(("parts", "ao"), ("blk", "sub"), None),
        P(("parts", "blk", "sub"), None),
        P(("parts", "blk", "sub"), None),
        P("parts", None),
        P("parts", None),
    )
    return jax.shard_map(
        body_pair if mesh.shape["ao"] == 2 else body_any,
        mesh=mesh,
        in_specs=placed,
        out_specs=P(("parts", "blk", "sub"), None, None),
        check_vma=False,
    )
```

time: 621 us -> 258 us (0.42)
  local copies, waits for them, and re-layouts: 339 us -> 5.37 us
  blocking collectives: 135 us -> 8.85 us
  Pallas kernels: 0 us -> 90.4 us
  waiting for transfers between devices: 67.4 us -> 112 us
  matrix products: 41.1 us -> 0.41 us
  between operations: 0.17 us -> 13.6 us
  starting transfers between devices: 18.6 us -> 10.1 us
    mul x7 -> x2, local copies, waits for them, and re-layouts: 260 us -> 1.03 us  [mask_three(): return (shaped * wide[:, None, :, None, :]).reshape(three.shape)]
    all_to_all x1 -> x0, blocking collectives: 96.9 us -> none  [body(): lax.all_to_all(rounded, 'ao', split_axis=0, concat_axis=2, tiled=True)]
    pallas_call x0 -> x12, Pallas kernels: none -> 90.4 us  [the longest x8 50.2 us: band(): pl.pallas_call(band_kernel, grid=(half // rows,), out_shape=jax.ShapeDtyp...]
    ppermute x4 -> x7, waiting for transfers between devices: 0.02 us -> 84 us  [the longest x1 60.1 us: body_pair(): oth = lax.ppermute(jnp.where(first, high, low), 'ao', swap)]
    all_to_all x1 -> x0, waiting for transfers between devices: 67.4 us -> none  [body(): lax.all_to_all(left, 'ao', split_axis=2, concat_axis=0, tiled=True)]
    dot_general x5 -> x3, matrix products: 41.1 us -> 0.41 us  [widen_last(): jnp.dot(flat, spread(count, size), preferred_element_type=jnp.float32)]
    all_to_all x3 -> x0, local copies, waits for them, and re-layouts: 36 us -> none  [the longest x2 22.3 us: body(): lax.all_to_all(rounded, 'ao', split_axis=0, concat_axis=2, tiled=True)]
    reshape x3 -> x1, local copies, waits for them, and re-layouts: 30.8 us -> 0.09 us  [body_pair(): return lax.psum(chi, 'ao').reshape(aux, 3, aux)]
  transfers between devices with their start and end apart: 5 -> 8, of which waited for: 1 -> 4; matrix products, arithmetic and copies ran while one was open for 26% -> 4% of each run, Pallas kernels for 0% -> 33%
where the time goes in v1:
time: 258 us; the launch traced here: 255 us
  waiting for transfers between devices  112 us (43%)
  Pallas kernels  90.4 us (35%)
  other arithmetic  14.2 us (6%)
  between operations  13.6 us (5%)
  starting transfers between devices  10.1 us (4%)
  blocking collectives  8.85 us (3%)
  local copies, waits for them, and re-layouts  5.37 us (2%)
    ppermute x1, waiting for transfers between devices, body_pair(): oth = lax.ppermute(jnp.where(first, high, low), 'ao', swap)  60.1 us
    pallas_call x8, Pallas kernels, band(): pl.pallas_call(band_kernel, grid=(half // rows,), out_shape=jax.ShapeDtyp...  50.2 us
    pallas_call x4, Pallas kernels, transform(): pl.pallas_call(transform_kernel, out_shape=(out, out), in_specs=[vmem] *...  40.2 us
    all_gather x1, waiting for transfers between devices, body_pair(): lax.all_gather(jnp.stack([g_occ, g_virt]), ('blk', 'sub'), axis=1, tiled=...  28.1 us
    ppermute x4, waiting for transfers between devices, body_pair(): recv = lax.ppermute(send, 'ao', swap)  23.9 us
    psum x1, blocking collectives, body_pair(): return lax.psum(chi, 'ao').reshape(aux, 3, aux)  8.85 us
    select_n x1, other arithmetic, body_pair(): oth = lax.ppermute(jnp.where(first, high, low), 'ao', swap)  5.78 us
    mul x1, other arithmetic, mask_three(): return (shaped * wide[:, None, :, None, :]).reshape(three.shape)  5.28 us
  transfers between devices with their start and end apart: 8, of which 4 were waited for; matrix products, arithmetic and copies ran while one was open for 4% of the time, Pallas kernels for 33%

profile of v1, /device:TPU:8, one launch (start us, length us, event | category | flops | bytes accessed | tf_op | source)
XLA Modules:
  0.0 255.0 jit_solution(11630860233098154070)
XLA Ops:
  6.5 0.7 convert_element_type.30
  7.5 1.0 mul.38
  8.5 2.4 copy-done
  10.8 5.3 %mul.40.here_ref = bf16[256,32,512]{2,1,0:T(8,128)(2,1)} multiply(bf16[256,32,512]{2,1,0:T(8,128)(2,1)S(1)} %copy-done, bf16[256,32,512]{2,1,0:T(8,128)(2,1)S(1)} %bitcast.26) | non-fusion elementwise | flops 4194304 | bytes 25165824 | tf_op jit(solution)/shard_map/mul | solution.py:43
  16.1 1.9 collective-permute-start.2
  18.0 2.4 collective-permute-start.1
  20.5 5.8 %broadcast_select_fusion = (bf16[256,16,512]{2,1,0:T(8,128)(2,1)}, bf16[256,16,512]{2,1,0:T(8,128)(2,1)}) fusion(pred[]{:T(512)S(6)} %eq.12, bf16[256,32,512]{2,1,0:T(8,128)(2,1)} %mul.40.here_ref), kind=kLoop, calls=%fused_computation | loop fusion | flops 4194304 | bytes 16777216 | tf_op jit(solution)/shard_map/jit(_where)/select_n | solution.py:155
  26.3 1.5 collective-permute-start
  27.8 0.7 pad_maximum_fusion
  28.8 28.1 %all-gather.2.cloned.1.call-done = bf16[2,512,512]{2,1,0:T(8,128)(2,1)} async-done(((bf16[2,64,512]{2,1,0:T(8,128)(2,1)}), bf16[2,512,512]{2,1,0:T(8,128)(2,1)}) %all-gather.2.cloned.1.call-update) | async-done | bytes 1048592 | tf_op jit(solution)/shard_map/all_gather | solution.py:156
  56.8 1.1 slice.60
  58.0 1.5 maximum_select_fusion
  59.8 60.1 %collective-permute-done.oth_ref = bf16[256,16,512]{2,1,0:T(8,128)(2,1)} collective-permute-done((bf16[256,16,512]{2,1,0:T(8,128)(2,1)}, bf16[256,16,512]{2,1,0:T(8,128)(2,1)}, u32[]{:S(2)}, u32[]{:S(2)}) %collective-permute-start) | collective-permute-done | bytes 4194336 | tf_op jit(solution)/shard_map/ppermute | solution.py:155
  119.8 10.0 %transform.7 = (bf16[256,16,128]{2,1,0:T(8,128)(2,1)S(1)}, bf16[256,16,128]{2,1,0:T(8,128)(2,1)S(1)}) custom-call(bf16[256,16,512]{2,1,0:T(8,128)(2,1)} %get-tuple-element.22.own_ref, bf16[256,16,512]{2,1,0:T(8,128)(2,1)} %collective-permute-done.oth_ref, bf16[512,128]{1,0:T(8,128)(2,1)S(1)} %get-tuple-element.26.occ_ref, ...), custom_call_target="tpu_custom_call" | custom-call | flops 4294967296 | bytes 10485760 | tf_op jit(solution)/shard_map/transform/pallas_call | solution.py:86
  129.8 1.6 collective-permute-start.6
  131.4 10.0 %transform.6 = (bf16[256,16,128]{2,1,0:T(8,128)(2,1)S(1)}, bf16[256,16,128]{2,1,0:T(8,128)(2,1)S(1)}) custom-call(bf16[256,16,512]{2,1,0:T(8,128)(2,1)} %get-tuple-element.22.own_ref, bf16[256,16,512]{2,1,0:T(8,128)(2,1)} %collective-permute-done.oth_ref, bf16[512,128]{1,0:T(8,128)(2,1)S(1)} %get-tuple-element.27.occ_ref, ...), custom_call_target="tpu_custom_call" | custom-call | flops 4294967296 | bytes 10485760 | tf_op jit(solution)/shard_map/transform/pallas_call | solution.py:86
  141.4 0.6 collective-permute-start.5
  142.0 10.0 %transform.5 = (bf16[256,16,128]{2,1,0:T(8,128)(2,1)S(1)}, bf16[256,16,128]{2,1,0:T(8,128)(2,1)S(1)}) custom-call(bf16[256,16,512]{2,1,0:T(8,128)(2,1)} %get-tuple-element.22.own_ref, bf16[256,16,512]{2,1,0:T(8,128)(2,1)} %collective-permute-done.oth_ref, bf16[512,128]{1,0:T(8,128)(2,1)S(1)} %get-tuple-element.25.occ_ref, ...), custom_call_target="tpu_custom_call" | custom-call | flops 4294967296 | bytes 10485760 | tf_op jit(solution)/shard_map/transform/pallas_call | solution.py:86
  152.0 1.6 collective-permute-start.4
  153.6 10.2 %transform.4 = (bf16[256,16,128]{2,1,0:T(8,128)(2,1)S(1)}, bf16[256,16,128]{2,1,0:T(8,128)(2,1)S(1)}) custom-call(bf16[256,16,512]{2,1,0:T(8,128)(2,1)} %get-tuple-element.22.own_ref, bf16[256,16,512]{2,1,0:T(8,128)(2,1)} %collective-permute-done.oth_ref, bf16[512,128]{1,0:T(8,128)(2,1)S(1)} %get-tuple-element.28.occ_ref, ...), custom_call_target="tpu_custom_call" | custom-call | flops 4294967296 | bytes 10485760 | tf_op jit(solution)/shard_map/transform/pallas_call | solution.py:86
  164.4 6.3 %band.15 = f32[16,96]{1,0:T(8,128)S(1)} custom-call(bf16[256,16,128]{2,1,0:T(8,128)(2,1)S(1)} %collective-permute-done.6.right_ref, bf16[256,32,512]{2,1,0:T(8,128)(2,1)} %collective-permute-done.1.before_ref, bf16[256,32,512]{2,1,0:T(8,128)(2,1)} %mul.40.here_ref, bf16[256,32,512]{2,1,0:T(8,128)(2,1)} %collective-permute-done.2.after_ref), custom_call_target="tpu_custom_call" | custom-call | flops 805306368 | bytes 7340032 | tf_op jit(solution)/shard_map/band/pallas_call | solution.py:130
  170.6 7.7 %collective-permute-done.5.right_ref = bf16[256,16,128]{2,1,0:T(8,128)(2,1)S(1)} collective-permute-done((bf16[256,16,128]{2,1,0:T(8,128)(2,1)S(1)}, bf16[256,16,128]{2,1,0:T(8,128)(2,1)S(1)}, u32[]{:S(2)}, u32[]{:S(2)}) %collective-permute-start.5) | collective-permute-done | bytes 1048608 | tf_op jit(solution)/shard_map/ppermute | solution.py:165
  178.3 6.3 %band.14 = f32[16,96]{1,0:T(8,128)S(1)} custom-call(bf16[256,16,128]{2,1,0:T(8,128)(2,1)S(1)} %collective-permute-done.5.right_ref, bf16[256,32,512]{2,1,0:T(8,128)(2,1)} %collective-permute-done.1.before_ref, bf16[256,32,512]{2,1,0:T(8,128)(2,1)} %mul.40.here_ref, bf16[256,32,512]{2,1,0:T(8,128)(2,1)} %collective-permute-done.2.after_ref), custom_call_target="tpu_custom_call" | custom-call | flops 805306368 | bytes 7340032 | tf_op jit(solution)/shard_map/band/pallas_call | solution.py:130
  184.6 16.2 %collective-permute-done.4.right_ref = bf16[256,16,128]{2,1,0:T(8,128)(2,1)S(1)} collective-permute-done((bf16[256,16,128]{2,1,0:T(8,128)(2,1)S(1)}, bf16[256,16,128]{2,1,0:T(8,128)(2,1)S(1)}, u32[]{:S(2)}, u32[]{:S(2)}) %collective-permute-start.4) | collective-permute-done | bytes 1048608 | tf_op jit(solution)/shard_map/ppermute | solution.py:165
  200.8 6.3 %band.13 = f32[16,96]{1,0:T(8,128)S(1)} custom-call(bf16[256,16,128]{2,1,0:T(8,128)(2,1)S(1)} %collective-permute-done.4.right_ref, bf16[256,32,512]{2,1,0:T(8,128)(2,1)} %collective-permute-done.1.before_ref, bf16[256,32,512]{2,1,0:T(8,128)(2,1)} %mul.40.here_ref, bf16[256,32,512]{2,1,0:T(8,128)(2,1)} %collective-permute-done.2.after_ref), custom_call_target="tpu_custom_call" | custom-call | flops 805306368 | bytes 7340032 | tf_op jit(solution)/shard_map/band/pallas_call | solution.py:130
  207.1 6.3 %band.11 = f32[16,96]{1,0:T(8,128)S(1)} custom-call(bf16[256,16,128]{2,1,0:T(8,128)(2,1)S(1)} %get-tuple-element.16.right_ref, bf16[256,32,512]{2,1,0:T(8,128)(2,1)} %collective-permute-done.1.before_ref, bf16[256,32,512]{2,1,0:T(8,128)(2,1)} %mul.40.here_ref, bf16[256,32,512]{2,1,0:T(8,128)(2,1)} %collective-permute-done.2.after_ref), custom_call_target="tpu_custom_call" | custom-call | flops 805306368 | bytes 7340032 | tf_op jit(solution)/shard_map/band/pallas_call | solution.py:130
  213.4 6.3 %band.10 = f32[16,96]{1,0:T(8,128)S(1)} custom-call(bf16[256,16,128]{2,1,0:T(8,128)(2,1)S(1)} %get-tuple-element.15.right_ref, bf16[256,32,512]{2,1,0:T(8,128)(2,1)} %collective-permute-done.1.before_ref, bf16[256,32,512]{2,1,0:T(8,128)(2,1)} %mul.40.here_ref, bf16[256,32,512]{2,1,0:T(8,128)(2,1)} %collective-permute-done.2.after_ref), custom_call_target="tpu_custom_call" | custom-call | flops 805306368 | bytes 7340032 | tf_op jit(solution)/shard_map/band/pallas_call | solution.py:130
  219.6 6.3 %band.9 = f32[16,96]{1,0:T(8,128)S(1)} custom-call(bf16[256,16,128]{2,1,0:T(8,128)(2,1)S(1)} %get-tuple-element.14.right_ref, bf16[256,32,512]{2,1,0:T(8,128)(2,1)} %collective-permute-done.1.before_ref, bf16[256,32,512]{2,1,0:T(8,128)(2,1)} %mul.40.here_ref, bf16[256,32,512]{2,1,0:T(8,128)(2,1)} %collective-permute-done.2.after_ref), custom_call_target="tpu_custom_call" | custom-call | flops 805306368 | bytes 7340032 | tf_op jit(solution)/shard_map/band/pallas_call | solution.py:130
  225.9 6.3 %band.8 = f32[16,96]{1,0:T(8,128)S(1)} custom-call(bf16[256,16,128]{2,1,0:T(8,128)(2,1)S(1)} %get-tuple-element.13.right_ref, bf16[256,32,512]{2,1,0:T(8,128)(2,1)} %collective-permute-done.1.before_ref, bf16[256,32,512]{2,1,0:T(8,128)(2,1)} %mul.40.here_ref, bf16[256,32,512]{2,1,0:T(8,128)(2,1)} %collective-permute-done.2.after_ref), custom_call_target="tpu_custom_call" | custom-call | flops 805306368 | bytes 7340032 | tf_op jit(solution)/shard_map/band/pallas_call | solution.py:130
  232.3 6.3 %band.12 = f32[16,96]{1,0:T(8,128)S(1)} custom-call(bf16[256,16,128]{2,1,0:T(8,128)(2,1)S(1)} %collective-permute-done.3.right_ref, bf16[256,32,512]{2,1,0:T(8,128)(2,1)} %collective-permute-done.1.before_ref, bf16[256,32,512]{2,1,0:T(8,128)(2,1)} %mul.40.here_ref, bf16[256,32,512]{2,1,0:T(8,128)(2,1)} %collective-permute-done.2.after_ref), custom_call_target="tpu_custom_call" | custom-call | flops 805306368 | bytes 7340032 | tf_op jit(solution)/shard_map/band/pallas_call | solution.py:130
  238.7 8.8 %psum.7 = f32[32,3,32]{2,1,0:T(4,128)S(1)} all-reduce(f32[32,3,32]{2,1,0:T(4,128)S(1)} %reshape.21), channel_id=1, replica_groups=mesh['parts'=2,'blk'=4,'ao'=2,'sub'=2] {'ao'}, use_global_device_ids=true, to_apply=%region_0.1 | all-reduce | flops 3072 | bytes 24576 | tf_op jit(solution)/shard_map/psum | solution.py:171
  247.5 0.6 copy.8
  (31 shorter events, 1.6 us)
Async XLA Ops:
  6.5 50.3 %all-gather.2.cloned.1.call-start = ((), (), s32[]{:S(2)}) async-start(), calls=%async_computation | async-start | bytes 1179648 | tf_op jit(solution)/shard_map/all_gather | solution.py:156
  7.4 3.4 %copy-start = (bf16[256,32,512]{2,1,0:T(8,128)(2,1)S(1)}, bf16[256,32,512]{2,1,0:T(8,128)(2,1)}, u32[]{:S(2)}) copy-start(bf16[256,32,512]{2,1,0:T(8,128)(2,1)} %param.6) | copy-start | bytes 25165828
  16.1 148.3 %collective-permute-start.2 = (bf16[256,32,512]{2,1,0:T(8,128)(2,1)}, bf16[256,32,512]{2,1,0:T(8,128)(2,1)}, u32[]{:S(2)}, u32[]{:S(2)}) collective-permute-start(bf16[256,32,512]{2,1,0:T(8,128)(2,1)} %mul.40.here_ref), channel_id=1, source_target_pairs={{1,0},{4,1},{5,4},{8,5},{9,8},{12,9},{13,12},{3,2},{6,3},{7,6},{10... | collective-permute-start | bytes 25165832 | tf_op jit(solution)/shard_map/ppermute | solution.py:17
  18.0 146.3 %collective-permute-start.1 = (bf16[256,32,512]{2,1,0:T(8,128)(2,1)}, bf16[256,32,512]{2,1,0:T(8,128)(2,1)}, u32[]{:S(2)}, u32[]{:S(2)}) collective-permute-start(bf16[256,32,512]{2,1,0:T(8,128)(2,1)} %mul.40.here_ref), channel_id=1, source_target_pairs={{0,1},{1,4},{4,5},{5,8},{8,9},{9,12},{12,13},{2,3},{3,6},{6,7},{7,... | collective-permute-start | bytes 25165832 | tf_op jit(solution)/shard_map/ppermute | solution.py:17
  20.4 7.3 %copy-start.1 = (bf16[64,512]{1,0:T(8,128)(2,1)S(1)}, bf16[64,512]{1,0:T(8,128)(2,1)}, u32[]{:S(2)}) copy-start(bf16[64,512]{1,0:T(8,128)(2,1)} %param.9) | copy-start | bytes 196612
  20.5 7.3 %copy-start.2 = (bf16[64,512]{1,0:T(8,128)(2,1)S(1)}, bf16[64,512]{1,0:T(8,128)(2,1)}, u32[]{:S(2)}) copy-start(bf16[64,512]{1,0:T(8,128)(2,1)} %param.8) | copy-start | bytes 196612
  20.5 8.0 %copy-start.3 = (s32[32,32]{1,0:T(8,128)S(1)}, s32[32,32]{1,0:T(8,128)}, u32[]{:S(2)}) copy-start(s32[32,32]{1,0:T(8,128)} %param.11) | copy-start | bytes 12292
  20.5 8.1 %copy-start.4 = (s32[32,32]{1,0:T(8,128)S(1)}, s32[32,32]{1,0:T(8,128)}, u32[]{:S(2)}) copy-start(s32[32,32]{1,0:T(8,128)} %param.10) | copy-start | bytes 12292
  26.3 93.5 %collective-permute-start = (bf16[256,16,512]{2,1,0:T(8,128)(2,1)}, bf16[256,16,512]{2,1,0:T(8,128)(2,1)}, u32[]{:S(2)}, u32[]{:S(2)}) collective-permute-start(bf16[256,16,512]{2,1,0:T(8,128)(2,1)} %get-tuple-element.21), channel_id=1, source_target_pairs={{0,2},{2,0},{1,3},{3,1},{4,6},{6,4},{5,7},{7,5},{8,10},{10,8},{9,1... | collective-permute-start | bytes 12582920 | tf_op jit(solution)/shard_map/ppermute | solution.py:155
  129.8 33.9 %collective-permute-start.6 = (bf16[256,16,128]{2,1,0:T(8,128)(2,1)S(1)}, bf16[256,16,128]{2,1,0:T(8,128)(2,1)S(1)}, u32[]{:S(2)}, u32[]{:S(2)}) collective-permute-start(bf16[256,16,128]{2,1,0:T(8,128)(2,1)S(1)} %get-tuple-element.20), channel_id=1, source_target_pairs={{0,2},{2,0},{1,3},{3,1},{4,6},{6,4},{5,7},{7,5},{8,10},{10,8},{9,1... | collective-permute-start | bytes 3145736 | tf_op jit(solution)/shard_map/ppermute | solution.py:165
  141.4 36.9 %collective-permute-start.5 = (bf16[256,16,128]{2,1,0:T(8,128)(2,1)S(1)}, bf16[256,16,128]{2,1,0:T(8,128)(2,1)S(1)}, u32[]{:S(2)}, u32[]{:S(2)}) collective-permute-start(bf16[256,16,128]{2,1,0:T(8,128)(2,1)S(1)} %get-tuple-element.19), channel_id=1, source_target_pairs={{0,2},{2,0},{1,3},{3,1},{4,6},{6,4},{5,7},{7,5},{8,10},{10,8},{9,1... | collective-permute-start | bytes 3145736 | tf_op jit(solution)/shard_map/ppermute | solution.py:165
  152.0 48.8 %collective-permute-start.4 = (bf16[256,16,128]{2,1,0:T(8,128)(2,1)S(1)}, bf16[256,16,128]{2,1,0:T(8,128)(2,1)S(1)}, u32[]{:S(2)}, u32[]{:S(2)}) collective-permute-start(bf16[256,16,128]{2,1,0:T(8,128)(2,1)S(1)} %get-tuple-element.18), channel_id=1, source_target_pairs={{0,2},{2,0},{1,3},{3,1},{4,6},{6,4},{5,7},{7,5},{8,10},{10,8},{9,1... | collective-permute-start | bytes 3145736 | tf_op jit(solution)/shard_map/ppermute | solution.py:165
  163.8 68.5 %collective-permute-start.3 = (bf16[256,16,128]{2,1,0:T(8,128)(2,1)S(1)}, bf16[256,16,128]{2,1,0:T(8,128)(2,1)S(1)}, u32[]{:S(2)}, u32[]{:S(2)}) collective-permute-start(bf16[256,16,128]{2,1,0:T(8,128)(2,1)S(1)} %get-tuple-element.17), channel_id=1, source_target_pairs={{0,2},{2,0},{1,3},{3,1},{4,6},{6,4},{5,7},{7,5},{8,10},{10,8},{9,1... | collective-permute-start | bytes 3145736 | tf_op jit(solution)/shard_map/ppermute | solution.py:165
Sparse Core Ops, SparseCore 0:
  28.6 28.1 all-gather.1

commit v2 on v1

--- a/solution.py
+++ b/solution.py
@@ -1,3 +1,5 @@
+import functools
+
 import jax
 import jax.numpy as jnp
 from jax import lax
@@ -8,7 +10,6 @@
 BS = 16
 ABLK = 16
 CHUNK = 128
-VMEM_LIMIT = 48 * 1024 * 1024
 
 
 def shift(x, axis, by):
@@ -43,24 +44,185 @@
     return (shaped * wide[:, None, :, None, :]).reshape(three.shape)
 
 
-def transform_kernel(own_ref, oth_ref, occ_ref, virt_ref, send_ref, keep_ref, left_ref, right_ref):
-    half, share, depth = own_ref.shape
+PARTS = 4
+
+
+def front_kernel(
+    three_ref, wide_ref, eff_ref, oth_ref, before_ref, after_ref, held, load_sem, store_sem,
+    edge_sem, pair_send, pair_recv, up_send, up_recv, down_send, down_recv,
+):
+    half, aux, depth = held.shape
+    share = aux // 2
+    part = half // PARTS
+    subs = lax.axis_size("sub")
+    count = lax.axis_size("blk") * subs
+    me = lax.axis_index("blk") * subs + lax.axis_index("sub")
+    ao = lax.axis_index("ao")
+    above = jnp.minimum(me + 1, count - 1)
+    below = jnp.maximum(me - 1, 0)
+    pair_id = {"ao": 1 - ao}
+    above_id = {"blk": above // subs, "sub": above % subs}
+    below_id = {"blk": below // subs, "sub": below % subs}
+    has_above, has_below = me < count - 1, me > 0
+    spans = [pl.ds(k * part, part) for k in range(PARTS)]
+
+    loads = [
+        pltpu.make_async_copy(three_ref.at[s], held.at[s], load_sem.at[k])
+        for k, s in enumerate(spans)
+    ]
+    for copy in loads:
+        copy.start()
+    barrier = pltpu.get_barrier_semaphore()
+    pl.semaphore_signal(barrier, inc=1, device_id=pair_id, device_id_type=pl.DeviceIdType.MESH)
+
+    @pl.when(has_above)
+    def _():
+        pl.semaphore_signal(
+            barrier, inc=1, device_id=above_id, device_id_type=pl.DeviceIdType.MESH
+        )
+
+    @pl.when(has_below)
+    def _():
+        pl.semaphore_signal(
+            barrier, inc=1, device_id=below_id, device_id_type=pl.DeviceIdType.MESH
+        )
+
+    theirs = pl.ds(pl.multiple_of((1 - ao) * share, share), share)
+
+    def remote(src, dst, send, recv, k, device):
+        return pltpu.make_async_remote_copy(
+            src_ref=src,
+            dst_ref=dst,
+            send_sem=send.at[k],
+            recv_sem=recv.at[k],
+            device_id=device,
+            device_id_type=pl.DeviceIdType.MESH,
+        )
+
+    pairs = [
+        remote(held.at[s, theirs], oth_ref.at[s], pair_send, pair_recv, k, pair_id)
+        for k, s in enumerate(spans)
+    ]
+    ups = [
+        remote(held.at[s], before_ref.at[s], up_send, up_recv, k, above_id)
+        for k, s in enumerate(spans)
+    ]
+    downs = [
+        remote(held.at[s], after_ref.at[s], down_send, down_recv, k, below_id)
+        for k, s in enumerate(spans)
+    ]
+    stores = [
+        pltpu.make_async_copy(held.at[s], eff_ref.at[s], store_sem.at[k])
+        for k, s in enumerate(spans)
+    ]
+    for k in range(PARTS):
+        loads[k].wait()
+
+        @pl.loop(0, part // BS)
+        def _(i, k=k):
+            row = k * (part // BS) + i
+            for j in range(aux // ABLK):
+                mask = wide_ref[pl.ds(row * (aux // ABLK) + j, 1), :].astype(jnp.bfloat16)
+                at = (pl.ds(row * BS, BS), pl.ds(j * ABLK, ABLK))
+                held[at] = held[at] * mask[None]
+
+        if k == 0:
+            pl.semaphore_wait(
+                barrier, 1 + has_above.astype(jnp.int32) + has_below.astype(jnp.int32)
+            )
+        pairs[k].start()
+
+        @pl.when(has_above)
+        def _(k=k):
+            ups[k].start()
+
+        @pl.when(has_below)
+        def _(k=k):
+            downs[k].start()
+
+        stores[k].start()
+
+    @pl.when(jnp.logical_not(has_below))
+    def _():
+        copy = pltpu.make_async_copy(held, before_ref, edge_sem.at[0])
+        copy.start()
+        copy.wait()
+
+    @pl.when(jnp.logical_not(has_above))
+    def _():
+        copy = pltpu.make_async_copy(held, after_ref, edge_sem.at[1])
+        copy.start()
+        copy.wait()
+
+    for k in range(PARTS):
+        stores[k].wait()
+
+        @pl.when(has_above)
+        def _(k=k):
+            ups[k].wait_send()
+            downs[k].wait_recv()
+
+        @pl.when(has_below)
+        def _(k=k):
+            downs[k].wait_send()
+            ups[k].wait_recv()
+
+        pairs[k].wait()
+
+
+def front(three, wide):
+    half, aux, depth = three.shape
+    hbm = pl.BlockSpec(memory_space=pl.ANY)
+    whole = jax.ShapeDtypeStruct(three.shape, three.dtype)
+    part = jax.ShapeDtypeStruct((half, aux // 2, depth), three.dtype)
+    return pl.pallas_call(
+        front_kernel,
+        out_shape=(whole, part, whole, whole),
+        in_specs=[hbm, pl.BlockSpec(memory_space=pltpu.VMEM)],
+        out_specs=(hbm,) * 4,
+        scratch_shapes=[pltpu.VMEM(three.shape, three.dtype)]
+        + [pltpu.SemaphoreType.DMA((PARTS,))] * 2
+        + [pltpu.SemaphoreType.DMA((2,))]
+        + [pltpu.SemaphoreType.DMA((PARTS,))] * 6,
+        compiler_params=pltpu.CompilerParams(
+            collective_id=0, has_side_effects=True, vmem_limit_bytes=16 * 1024 * 1024
+        ),
+        cost_estimate=pl.CostEstimate(
+            flops=10**11, bytes_accessed=10 * half * aux * depth, transcendentals=0
+        ),
+        name="front",
+    )(three, wide)
+
+
+def transform_kernel(has_sum, last, *refs):
+    pieces = refs[: len(refs) - 5 - has_sum - last]
+    refs = refs[len(pieces) :]
+    occ_ref, virt_ref, sum_ref = refs[0], refs[1], refs[2] if has_sum else None
+    out_refs = refs[2 + has_sum : -2]
+    left_ref, right_ref = refs[-2:]
+    if not last:
+        right_ref = out_refs[0]
+    share, depth = pieces[0].shape[1:]
     width = occ_ref.shape[1]
-    full = 2 * half
+    have, full = virt_ref.shape
+    half = full // 2
     step = 64
     occ = occ_ref[...]
-    for which, ref in enumerate((own_ref, oth_ref)):
-
-        @pl.loop(0, half // step)
-        def _(i, ref=ref, which=which):
+    base = 0
+    for ref in pieces:
+
+        @pl.loop(0, ref.shape[0] // step)
+        def _(i, ref=ref, base=base):
             rows = ref[pl.ds(i * step, step)].reshape(step * share, depth)
-            at = pl.multiple_of((which * half + i * step) * share, step * share)
+            at = pl.multiple_of((base + i * step) * share, step * share)
             left_ref[pl.ds(at, step * share), :] = jnp.dot(
                 rows, occ, preferred_element_type=jnp.float32
             )
 
+        base += ref.shape[0]
+
     for p in range(0, share, 2):
-        pair = [left_ref[pl.ds(p + k, full, stride=share), :].astype(jnp.bfloat16) for k in (0, 1)]
+        pair = [left_ref[pl.ds(p + k, have, stride=share), :].astype(jnp.bfloat16) for k in (0, 1)]
         out = lax.dot_general(
             virt_ref[...],
             jnp.concatenate(pair, axis=1),
@@ -69,34 +231,46 @@
         )
         for k in (0, 1):
             right_ref[pl.ds(p + k, full, stride=share), :] = out[:, k * width : (k + 1) * width]
-    for which, ref in enumerate((send_ref, keep_ref)):
+    if not last:
+        return
+    for which, ref in enumerate(out_refs):
 
         @pl.loop(0, half // step)
         def _(i, ref=ref, which=which):
             at = pl.multiple_of((which * half + i * step) * share, step * share)
-            rows = right_ref[pl.ds(at, step * share), :].astype(jnp.bfloat16)
-            ref[pl.ds(i * step, step)] = rows.reshape(step, share, width)
-
-
-def transform(own, oth, occ, virt):
-    half, share, depth = own.shape
+            rows = right_ref[pl.ds(at, step * share), :]
+            if has_sum:
+                rows += sum_ref[pl.ds(at, step * share), :]
+            ref[pl.ds(i * step, step)] = rows.astype(jnp.bfloat16).reshape(step, share, width)
+
+
+def transform(pieces, occ, virt, before=None, last=True):
+    have, full = virt.shape
+    share, depth = pieces[0].shape[1:]
     width = occ.shape[1]
-    out = jax.ShapeDtypeStruct((half, share, width), jnp.bfloat16)
+    if last:
+        out = (jax.ShapeDtypeStruct((full // 2, share, width), jnp.bfloat16),) * 2
+    else:
+        out = (jax.ShapeDtypeStruct((full * share, width), jnp.float32),)
     vmem = pl.BlockSpec(memory_space=pltpu.VMEM)
+    operands = (*pieces, occ, virt) + (() if before is None else (before,))
     return pl.pallas_call(
-        transform_kernel,
-        out_shape=(out, out),
-        in_specs=[vmem] * 4,
-        out_specs=(vmem, vmem),
-        scratch_shapes=[pltpu.VMEM((2 * half * share, width), jnp.float32)] * 2,
-        compiler_params=pltpu.CompilerParams(vmem_limit_bytes=VMEM_LIMIT),
+        functools.partial(transform_kernel, int(before is not None), int(last)),
+        out_shape=out,
+        in_specs=[vmem] * len(operands),
+        out_specs=(vmem,) * len(out),
+        scratch_shapes=[
+            pltpu.VMEM((have * share, width), jnp.float32),
+            pltpu.VMEM((full * share, width) if last else (8, width), jnp.float32),
+        ],
+        compiler_params=pltpu.CompilerParams(vmem_limit_bytes=32 * 1024 * 1024),
         cost_estimate=pl.CostEstimate(
-            flops=4 * half * share * width * (depth + 2 * half) * 2,
-            bytes_accessed=4 * half * share * depth + 4 * half * share * width,
+            flops=10 * have * share * width * (depth + full),
+            bytes_accessed=2 * have * share * depth + 4 * full * share * width,
             transcendentals=0,
         ),
         name="transform",
-    )(own, oth, occ, virt)
+    )(*operands)
 
 
 def band_kernel(right_ref, before_ref, here_ref, after_ref, out_ref):
@@ -122,20 +296,20 @@
     out_ref[...] += total
 
 
-def band(right, threes, chunk):
+def band(right, threes, chunk, start=0):
     half, share, width = right.shape
     aux = threes[0].shape[1]
     rows = 32
-    block = pl.BlockSpec((rows, aux, width), lambda i: (i, 0, chunk))
+    block = pl.BlockSpec((rows, aux, width), lambda i: (i + start // rows, 0, chunk))
     return pl.pallas_call(
         band_kernel,
         grid=(half // rows,),
         out_shape=jax.ShapeDtypeStruct((share, 3 * aux), jnp.float32),
         in_specs=[pl.BlockSpec((rows, share, width), lambda i: (i, 0, 0))] + [block] * 3,
         out_specs=pl.BlockSpec((share, 3 * aux), lambda i: (0, 0)),
-        compiler_params=pltpu.CompilerParams(vmem_limit_bytes=VMEM_LIMIT),
+        compiler_params=pltpu.CompilerParams(vmem_limit_bytes=16 * 1024 * 1024),
         cost_estimate=pl.CostEstimate(
-            flops=2 * half * share * 3 * aux * width * 8,
+            flops=2 * half * share * 3 * aux * width * 64,
             bytes_accessed=2 * half * width * (share + 3 * aux),
             transcendentals=0,
         ),
@@ -148,27 +322,40 @@
     share = aux // 2
     me = lax.axis_index("ao")
     swap = [(0, 1), (1, 0)]
-    eff = mask_three(three, three_mask)
-    low, high = eff[:, :share], eff[:, share:]
     first = me == 0
-    own = jnp.where(first, low, high)
-    oth = lax.ppermute(jnp.where(first, high, low), "ao", swap)
     both = lax.all_gather(jnp.stack([g_occ, g_virt]), ("blk", "sub"), axis=1, tiled=True)
+    wide = widen_last(three_mask, depth).reshape(-1, depth).astype(jnp.float32)
+    eff, oth, before, after = front(three, wide)
+    threes = (before, eff, after)
+    own = jnp.where(first, eff[:, :share], eff[:, share:])
     occ = mask_green(both[0], occ_mask)
     virt = mask_green(both[1], virt_mask)
-    rows = jnp.where(first, virt, jnp.concatenate([virt[half:], virt[:half]], axis=0))
-    virt = jnp.where(first, jnp.concatenate([rows[:, half:], rows[:, :half]], axis=1), rows)
-    threes = (shift(eff, ("blk", "sub"), 1), eff, shift(eff, ("blk", "sub"), -1))
-    kept, got = 0.0, 0.0
-    for c in range(depth // CHUNK):
-        send, keep = transform(own, oth, occ[:, c * CHUNK : (c + 1) * CHUNK], virt)
-        recv = lax.ppermute(send, "ao", swap)
+    virt = jnp.where(first, virt, jnp.concatenate([virt[half:], virt[:half]], axis=0))
+    virt = jnp.where(first, jnp.concatenate([virt[:, half:], virt[:, :half]], axis=1), virt)
+    kept, returned = 0.0, []
+    chunks = depth // CHUNK
+    for c in range(chunks):
+        occ_c = occ[:, c * CHUNK : (c + 1) * CHUNK]
+        send, keep = transform((own, oth), occ_c, virt)
+        send, own, virt = lax.optimization_barrier((send, own, virt))
+        cuts = (0, half) if c < chunks - 1 else (0, half // 2, half)
+        for start, stop in zip(cuts, cuts[1:]):
+            returned.append((lax.ppermute(send[start:stop], "ao", swap), c, start))
         kept = kept + band(keep, threes, c)
-        got = got + band(recv, threes, c)
+    got = 0.0
+    for recv, c, start in returned:
+        if c == chunks - 1:
+            recv, kept = lax.optimization_barrier((recv, kept))
+        got = got + band(recv, threes, c, start)
     chi = jnp.where(
         first, jnp.concatenate([kept, got], axis=0), jnp.concatenate([got, kept], axis=0)
     )
-    return lax.psum(chi, "ao").reshape(aux, 3, aux)
+    chi = chi + lax.ppermute(chi, "ao", swap)
+    tiles = chi.reshape(aux, 3, aux)
+    index = lax.axis_index(("blk", "sub"))
+    offset = index - 1 + lax.broadcasted_iota(jnp.int32, tiles.shape, 1)
+    inside = jnp.logical_and(offset >= 0, offset < lax.axis_size(("blk", "sub")))
+    return jnp.where(inside, tiles, 0.0)
 
 
 def body_any(three, three_mask, g_occ, g_virt, occ_mask, virt_mask):

time: 258 us -> 253 us (0.981); the launches traced: 255 us -> 253 us
  waiting for transfers between devices: 112 us -> 35.1 us
  Pallas kernels: 90.4 us -> 160 us
  local copies, waits for them, and re-layouts: 5.37 us -> 26.9 us
  blocking collectives: 8.85 us -> 0 us
  other arithmetic: 14.2 us -> 9.32 us
  starting transfers between devices: 10.1 us -> 7.13 us
    pallas_call x4 -> x5, Pallas kernels: 40.2 us -> 131 us  [the longest x1 102 us: front(): pl.pallas_call(front_kernel, out_shape=(whole, part, whole, whole), in_sp...]
    ppermute x7 -> x6, waiting for transfers between devices: 84 us -> 35.1 us  [the longest x5 32.7 us: body_pair(): returned.append((lax.ppermute(send[start:stop], 'ao', swap), c, start))]
    all_gather x1, waiting for transfers between devices: 28.1 us -> 0.01 us  [body_pair(): lax.all_gather(jnp.stack([g_occ, g_virt]), ('blk', 'sub'), axis=1, tiled=...]
    unnamed x10 -> x36, local copies, waits for them, and re-layouts: 2.39 us -> 24.7 us
    pallas_call x8 -> x9, Pallas kernels: 50.2 us -> 29.8 us  [band(): pl.pallas_call(band_kernel, grid=(half // rows,), out_shape=jax.ShapeDtyp...]
    psum x1 -> x0, blocking collectives: 8.85 us -> none  [body_pair(): return lax.psum(chi, 'ao').reshape(aux, 3, aux)]
    mul x1 -> x0, other arithmetic: 5.28 us -> none  [mask_three(): return (shaped * wide[:, None, :, None, :]).reshape(three.shape)]
    ppermute x7 -> x6, starting transfers between devices: 10.1 us -> 7.13 us  [the longest x5 5.72 us: body_pair(): returned.append((lax.ppermute(send[start:stop], 'ao', swap), c, start))]
  transfers between devices with their start and end apart: 8 -> 7, of which waited for: 4 -> 4; matrix products, arithmetic and copies ran while one was open for 4% -> 3% of each run, Pallas kernels for 33% -> 59%
where the time goes in v2:
time: 253 us
  Pallas kernels  160 us (63%)
  waiting for transfers between devices  35.1 us (14%)
  local copies, waits for them, and re-layouts  26.9 us (11%)
  between operations  13.6 us (5%)
  other arithmetic  9.32 us (4%)
  starting transfers between devices  7.13 us (3%)
    pallas_call x1, Pallas kernels, front(): pl.pallas_call(front_kernel, out_shape=(whole, part, whole, whole), in_sp...  102 us
    ppermute x5, waiting for transfers between devices, body_pair(): returned.append((lax.ppermute(send[start:stop], 'ao', swap), c, start))  32.7 us
    pallas_call x9, Pallas kernels, band(): pl.pallas_call(band_kernel, grid=(half // rows,), out_shape=jax.ShapeDtyp...  29.8 us
    pallas_call x4, Pallas kernels, transform(): pl.pallas_call(functools.partial(transform_kernel, int(before is not None...  28.3 us
    unnamed x36, local copies, waits for them, and re-layouts  24.7 us
    ppermute x5, starting transfers between devices, body_pair(): returned.append((lax.ppermute(send[start:stop], 'ao', swap), c, start))  5.72 us
    select_n x1, other arithmetic, body_pair(): own = jnp.where(first, eff[:, :share], eff[:, share:])  5.13 us
  transfers between devices with their start and end apart: 7, of which 4 were waited for; matrix products, arithmetic and copies ran while one was open for 3% of the time, Pallas kernels for 59%

profile of v2, /device:TPU:8, one launch (start us, length us, event | category | flops | bytes accessed | tf_op | source)
XLA Modules:
  0.0 252.7 jit_solution(7183510921559956837)
XLA Ops:
  6.5 1.5 pad_maximum_fusion
  9.0 3.4 %copy-done.6 = bf16[256,32,512]{2,1,0:T(8,128)(2,1)S(1)} copy-done((bf16[256,32,512]{2,1,0:T(8,128)(2,1)S(1)}, bf16[256,32,512]{2,1,0:T(8,128)(2,1)}, u32[]{:S(2)}) %copy-start.6) | copy-done | bytes 8388632
  12.4 102.2 %front.1 = (bf16[256,32,512]{2,1,0:T(8,128)(2,1)S(1)}, bf16[256,16,512]{2,1,0:T(8,128)(2,1)S(1)}, bf16[256,32,512]{2,1,0:T(8,128)(2,1)S(1)}, bf16[256,32,512]{2,1,0:T(8,128)(2,1)S(1)}) custom-call(bf16[256,32,512]{2,1,0:T(8,128)(2,1)S(1)} %copy-done.6, f32[32,512]{1,0:T(8,128)S(1)} %fusion.1.wide_ref), custom_call_target="tpu_custom_call" | custom-call | flops 99999997952 | bytes 41943040 | tf_op jit(solution)/shard_map/front/pallas_call | solution.py:178
  114.6 3.2 %copy-done = bf16[256,32,512]{2,1,0:T(8,128)(2,1)} copy-done((bf16[256,32,512]{2,1,0:T(8,128)(2,1)}, bf16[256,32,512]{2,1,0:T(8,128)(2,1)S(1)}, u32[]{:S(2)}) %copy-start) | copy-done | bytes 8388632
  117.8 3.3 %copy-done.1 = bf16[256,32,512]{2,1,0:T(8,128)(2,1)} copy-done((bf16[256,32,512]{2,1,0:T(8,128)(2,1)}, bf16[256,32,512]{2,1,0:T(8,128)(2,1)S(1)}, u32[]{:S(2)}) %copy-start.1) | copy-done | bytes 8388632
  121.1 3.3 %copy-done.2 = bf16[256,32,512]{2,1,0:T(8,128)(2,1)} copy-done((bf16[256,32,512]{2,1,0:T(8,128)(2,1)}, bf16[256,32,512]{2,1,0:T(8,128)(2,1)S(1)}, u32[]{:S(2)}) %copy-start.2) | copy-done | bytes 8388632
  124.4 2.0 copy-done.9
  126.7 5.1 %slice_select_fusion.refs_0_ = bf16[256,16,512]{2,1,0:T(8,128)(2,1)} fusion(bf16[256,32,512]{2,1,0:T(8,128)(2,1)} %copy-done, pred[]{:T(512)S(6)} %eq.12), kind=kLoop, calls=%fused_computation | loop fusion | flops 2097152 | bytes 12582913 | tf_op jit(solution)/shard_map/jit(_where)/select_n | solution.py:330
  133.0 1.6 maximum_select_fusion
  136.7 7.5 %transform.4 = (bf16[256,16,128]{2,1,0:T(8,128)(2,1)}, bf16[256,16,128]{2,1,0:T(8,128)(2,1)S(1)}) custom-call(bf16[256,16,512]{2,1,0:T(8,128)(2,1)S(1)} %copy-done.5, bf16[256,16,512]{2,1,0:T(8,128)(2,1)S(1)} %copy-done.10, bf16[512,128]{1,0:T(8,128)(2,1)S(1)} %get-tuple-element.64.refs_2_, bf16[512,512]{1,0:T(8,128)(2,1)S(1)} %maximum_select_fusion.1.refs_3_), custom_call_target="tpu_custom_call" | custom-call | flops 10737418240 | bytes 12582912 | tf_op jit(solution)/shard_map/transform/pallas_call | solution.py:257
  144.2 1.5 collective-permute-start.2
  145.7 7.5 %transform.5 = (bf16[256,16,128]{2,1,0:T(8,128)(2,1)}, bf16[256,16,128]{2,1,0:T(8,128)(2,1)S(1)}) custom-call(bf16[256,16,512]{2,1,0:T(8,128)(2,1)S(1)} %copy-done.5, bf16[256,16,512]{2,1,0:T(8,128)(2,1)S(1)} %copy-done.11, bf16[512,128]{1,0:T(8,128)(2,1)S(1)} %get-tuple-element.63.refs_2_, bf16[512,512]{1,0:T(8,128)(2,1)S(1)} %maximum_select_fusion.1.refs_3_), custom_call_target="tpu_custom_call" | custom-call | flops 10737418240 | bytes 12582912 | tf_op jit(solution)/shard_map/transform/pallas_call | solution.py:257
  153.3 3.4 %copy-done.3 = bf16[256,32,512]{2,1,0:T(8,128)(2,1)S(1)} copy-done((bf16[256,32,512]{2,1,0:T(8,128)(2,1)S(1)}, bf16[256,32,512]{2,1,0:T(8,128)(2,1)}, u32[]{:S(2)}) %copy-start.3) | copy-done | bytes 8388632
  156.7 3.7 %band.9 = f32[16,96]{1,0:T(8,128)S(1)} custom-call(bf16[256,16,128]{2,1,0:T(8,128)(2,1)S(1)} %get-tuple-element.44.right_ref, bf16[256,32,512]{2,1,0:T(8,128)(2,1)S(1)} %bitcast.28, bf16[256,32,512]{2,1,0:T(8,128)(2,1)S(1)} %bitcast.26, bf16[256,32,512]{2,1,0:T(8,128)(2,1)S(1)} %copy-done.3), custom_call_target="tpu_custom_call" | custom-call | flops 6442450944 | bytes 7340032 | tf_op jit(solution)/shard_map/band/pallas_call | solution.py:304
  160.4 3.7 %band.10 = f32[16,96]{1,0:T(8,128)S(1)} custom-call(bf16[256,16,128]{2,1,0:T(8,128)(2,1)S(1)} %get-tuple-element.47.right_ref, bf16[256,32,512]{2,1,0:T(8,128)(2,1)S(1)} %bitcast.28, bf16[256,32,512]{2,1,0:T(8,128)(2,1)S(1)} %bitcast.26, bf16[256,32,512]{2,1,0:T(8,128)(2,1)S(1)} %copy-done.3), custom_call_target="tpu_custom_call" | custom-call | flops 6442450944 | bytes 7340032 | tf_op jit(solution)/shard_map/band/pallas_call | solution.py:304
  164.7 6.6 %transform.6 = (bf16[256,16,128]{2,1,0:T(8,128)(2,1)S(1)}, bf16[256,16,128]{2,1,0:T(8,128)(2,1)S(1)}) custom-call(bf16[256,16,512]{2,1,0:T(8,128)(2,1)S(1)} %copy-done.5, bf16[256,16,512]{2,1,0:T(8,128)(2,1)S(1)} %copy-done.11, bf16[512,128]{1,0:T(8,128)(2,1)S(1)} %get-tuple-element.62.refs_2_, bf16[512,512]{1,0:T(8,128)(2,1)S(1)} %maximum_select_fusion.1.refs_3_), custom_call_target="tpu_custom_call" | custom-call | flops 10737418240 | bytes 12582912 | tf_op jit(solution)/shard_map/transform/pallas_call | solution.py:257
  172.2 6.7 %transform.7 = (bf16[256,16,128]{2,1,0:T(8,128)(2,1)S(1)}, bf16[256,16,128]{2,1,0:T(8,128)(2,1)S(1)}) custom-call(bf16[256,16,512]{2,1,0:T(8,128)(2,1)S(1)} %copy-done.5, bf16[256,16,512]{2,1,0:T(8,128)(2,1)S(1)} %copy-done.11, bf16[512,128]{1,0:T(8,128)(2,1)S(1)} %get-tuple-element.61.refs_2_, bf16[512,512]{1,0:T(8,128)(2,1)S(1)} %maximum_select_fusion.1.refs_3_), custom_call_target="tpu_custom_call" | custom-call | flops 10737418240 | bytes 12582912 | tf_op jit(solution)/shard_map/transform/pallas_call | solution.py:257
  179.2 3.4 %copy-done.4 = bf16[256,32,512]{2,1,0:T(8,128)(2,1)S(1)} copy-done((bf16[256,32,512]{2,1,0:T(8,128)(2,1)S(1)}, bf16[256,32,512]{2,1,0:T(8,128)(2,1)}, u32[]{:S(2)}) %copy-start.4) | copy-done | bytes 8388632
  182.5 3.7 %band.12 = f32[16,96]{1,0:T(8,128)S(1)} custom-call(bf16[256,16,128]{2,1,0:T(8,128)(2,1)S(1)} %get-tuple-element.49.right_ref, bf16[256,32,512]{2,1,0:T(8,128)(2,1)S(1)} %bitcast.28, bf16[256,32,512]{2,1,0:T(8,128)(2,1)S(1)} %bitcast.26, bf16[256,32,512]{2,1,0:T(8,128)(2,1)S(1)} %copy-done.4), custom_call_target="tpu_custom_call" | custom-call | flops 6442450944 | bytes 7340032 | tf_op jit(solution)/shard_map/band/pallas_call | solution.py:304
  186.2 1.6 collective-permute-start.1
  187.8 3.7 %band.11 = f32[16,96]{1,0:T(8,128)S(1)} custom-call(bf16[256,16,128]{2,1,0:T(8,128)(2,1)S(1)} %get-tuple-element.48.right_ref, bf16[256,32,512]{2,1,0:T(8,128)(2,1)S(1)} %bitcast.28, bf16[256,32,512]{2,1,0:T(8,128)(2,1)S(1)} %bitcast.26, bf16[256,32,512]{2,1,0:T(8,128)(2,1)S(1)} %copy-done.4), custom_call_target="tpu_custom_call" | custom-call | flops 6442450944 | bytes 7340032 | tf_op jit(solution)/shard_map/band/pallas_call | solution.py:304
  192.1 1.5 collective-permute-start.4
  193.6 10.2 %collective-permute-done.1.right_ref = bf16[128,16,128]{2,1,0:T(8,128)(2,1)S(1)} collective-permute-done((bf16[128,16,128]{2,1,0:T(8,128)(2,1)S(1)}, bf16[128,16,128]{2,1,0:T(8,128)(2,1)S(1)}, u32[]{:S(2)}, u32[]{:S(2)}) %collective-permute-start.1) | collective-permute-done | bytes 524320 | tf_op jit(solution)/shard_map/ppermute | solution.py:343
  203.8 1.9 band.16
  205.7 9.4 %collective-permute-done.right_ref = bf16[128,16,128]{2,1,0:T(8,128)(2,1)S(1)} collective-permute-done((bf16[128,16,128]{2,1,0:T(8,128)(2,1)S(1)}, bf16[128,16,128]{2,1,0:T(8,128)(2,1)S(1)}, u32[]{:S(2)}, u32[]{:S(2)}) %collective-permute-start) | collective-permute-done | bytes 524320 | tf_op jit(solution)/shard_map/ppermute | solution.py:343
  215.1 1.9 band.17
  216.9 3.7 %band.13 = f32[16,96]{1,0:T(8,128)S(1)} custom-call(bf16[256,16,128]{2,1,0:T(8,128)(2,1)S(1)} %collective-permute-done.2.right_ref, bf16[256,32,512]{2,1,0:T(8,128)(2,1)S(1)} %bitcast.28, bf16[256,32,512]{2,1,0:T(8,128)(2,1)S(1)} %bitcast.26, bf16[256,32,512]{2,1,0:T(8,128)(2,1)S(1)} %copy-done.4), custom_call_target="tpu_custom_call" | custom-call | flops 6442450944 | bytes 7340032 | tf_op jit(solution)/shard_map/band/pallas_call | solution.py:304
  220.7 3.7 %band.14 = f32[16,96]{1,0:T(8,128)S(1)} custom-call(bf16[256,16,128]{2,1,0:T(8,128)(2,1)S(1)} %collective-permute-done.3.right_ref, bf16[256,32,512]{2,1,0:T(8,128)(2,1)S(1)} %bitcast.28, bf16[256,32,512]{2,1,0:T(8,128)(2,1)S(1)} %bitcast.26, bf16[256,32,512]{2,1,0:T(8,128)(2,1)S(1)} %copy-done.4), custom_call_target="tpu_custom_call" | custom-call | flops 6442450944 | bytes 7340032 | tf_op jit(solution)/shard_map/band/pallas_call | solution.py:304
  224.4 13.1 %collective-permute-done.4.right_ref = bf16[256,16,128]{2,1,0:T(8,128)(2,1)S(1)} collective-permute-done((bf16[256,16,128]{2,1,0:T(8,128)(2,1)S(1)}, bf16[256,16,128]{2,1,0:T(8,128)(2,1)S(1)}, u32[]{:S(2)}, u32[]{:S(2)}) %collective-permute-start.4) | collective-permute-done | bytes 1048608 | tf_op jit(solution)/shard_map/ppermute | solution.py:343
  237.5 3.7 %band.15 = f32[16,96]{1,0:T(8,128)S(1)} custom-call(bf16[256,16,128]{2,1,0:T(8,128)(2,1)S(1)} %collective-permute-done.4.right_ref, bf16[256,32,512]{2,1,0:T(8,128)(2,1)S(1)} %bitcast.28, bf16[256,32,512]{2,1,0:T(8,128)(2,1)S(1)} %bitcast.26, bf16[256,32,512]{2,1,0:T(8,128)(2,1)S(1)} %copy-done.4), custom_call_target="tpu_custom_call" | custom-call | flops 6442450944 | bytes 7340032 | tf_op jit(solution)/shard_map/band/pallas_call | solution.py:304
  241.3 1.4 collective-permute-start.5
  242.7 2.4 collective-permute-done.5
  (59 shorter events, 7.5 us)
Async XLA Ops:
  6.5 125.3 %all-gather.2.cloned.1.call-start = ((), (), s32[]{:S(2)}) async-start(), calls=%async_computation | async-start | bytes 1179648 | tf_op jit(solution)/shard_map/all_gather | solution.py:326
  9.0 3.4 %copy-start.6 = (bf16[256,32,512]{2,1,0:T(8,128)(2,1)S(1)}, bf16[256,32,512]{2,1,0:T(8,128)(2,1)}, u32[]{:S(2)}) copy-start(bf16[256,32,512]{2,1,0:T(8,128)(2,1)} %three_ref.1) | copy-start | bytes 25165828
  12.4 114.1 %copy-start.12 = (s32[32,32]{1,0:T(8,128)S(1)}, s32[32,32]{1,0:T(8,128)}, u32[]{:S(2)}) copy-start(s32[32,32]{1,0:T(8,128)} %param.11) | copy-start | bytes 12292
  12.4 114.2 %copy-start.13 = (s32[32,32]{1,0:T(8,128)S(1)}, s32[32,32]{1,0:T(8,128)}, u32[]{:S(2)}) copy-start(s32[32,32]{1,0:T(8,128)} %param.10) | copy-start | bytes 12292
  114.6 3.3 %copy-start = (bf16[256,32,512]{2,1,0:T(8,128)(2,1)}, bf16[256,32,512]{2,1,0:T(8,128)(2,1)S(1)}, u32[]{:S(2)}) copy-start(bf16[256,32,512]{2,1,0:T(8,128)(2,1)S(1)} %get-tuple-element.31.here_ref) | copy-start | bytes 25165828
  117.8 3.3 %copy-start.1 = (bf16[256,32,512]{2,1,0:T(8,128)(2,1)}, bf16[256,32,512]{2,1,0:T(8,128)(2,1)S(1)}, u32[]{:S(2)}) copy-start(bf16[256,32,512]{2,1,0:T(8,128)(2,1)S(1)} %get-tuple-element.45.before_ref) | copy-start | bytes 25165828
  121.1 3.3 %copy-start.2 = (bf16[256,32,512]{2,1,0:T(8,128)(2,1)}, bf16[256,32,512]{2,1,0:T(8,128)(2,1)S(1)}, u32[]{:S(2)}) copy-start(bf16[256,32,512]{2,1,0:T(8,128)(2,1)S(1)} %get-tuple-element.46.after_ref) | copy-start | bytes 25165828
  124.4 2.0 copy-start.9
  132.9 2.5 copy-start.5
  132.9 3.8 %copy-start.10 = (bf16[256,16,512]{2,1,0:T(8,128)(2,1)S(1)}, bf16[256,16,512]{2,1,0:T(8,128)(2,1)}, u32[]{:S(2)}) copy-start(bf16[256,16,512]{2,1,0:T(8,128)(2,1)} %copy-done.9) | copy-start | bytes 12582916
  136.7 9.0 %copy-start.11 = (bf16[256,16,512]{2,1,0:T(8,128)(2,1)S(1)}, bf16[256,16,512]{2,1,0:T(8,128)(2,1)}, u32[]{:S(2)}) copy-start(bf16[256,16,512]{2,1,0:T(8,128)(2,1)} %copy-done.9) | copy-start | bytes 12582916
  136.7 16.6 %slice-start = ((s8[8388608]{0:T(1024)(128)(4,1)}), s8[4194304]{0:T(1024)(128)(4,1)S(1)}, s32[]{:S(2)}) async-start(s8[8388608]{0:T(1024)(128)(4,1)} %bitcast.25), calls=%async_computation.1 | async-start | bytes 8388608
  136.7 16.6 %slice-start.2 = ((s8[8388608]{0:T(1024)(128)(4,1)}), s8[4194304]{0:T(1024)(128)(4,1)S(1)}, s32[]{:S(2)}) async-start(s8[8388608]{0:T(1024)(128)(4,1)} %bitcast.27), calls=%async_computation.3 | async-start | bytes 8388608
  144.2 72.7 %collective-permute-start.2 = (bf16[256,16,128]{2,1,0:T(8,128)(2,1)}, bf16[256,16,128]{2,1,0:T(8,128)(2,1)S(1)}, u32[]{:S(2)}, u32[]{:S(2)}) collective-permute-start(bf16[256,16,128]{2,1,0:T(8,128)(2,1)} %get-tuple-element.52), channel_id=1, source_target_pairs={{0,2},{2,0},{1,3},{3,1},{4,6},{6,4},{5,7},{7,5},{8,10},{10,8},{9,1... | collective-permute-start | bytes 3145736 | tf_op jit(solution)/shard_map/ppermute | solution.py:343
  145.7 7.6 %slice-start.1 = ((s8[8388608]{0:T(1024)(128)(4,1)}), s8[4194304]{0:T(1024)(128)(4,1)S(1)}, s32[]{:S(2)}) async-start(s8[8388608]{0:T(1024)(128)(4,1)} %bitcast.25), calls=%async_computation.2 | async-start | bytes 8388608
  145.7 7.6 %slice-start.3 = ((s8[8388608]{0:T(1024)(128)(4,1)}), s8[4194304]{0:T(1024)(128)(4,1)S(1)}, s32[]{:S(2)}) async-start(s8[8388608]{0:T(1024)(128)(4,1)} %bitcast.27), calls=%async_computation.4 | async-start | bytes 8388608
  153.3 3.4 %copy-start.3 = (bf16[256,32,512]{2,1,0:T(8,128)(2,1)S(1)}, bf16[256,32,512]{2,1,0:T(8,128)(2,1)}, u32[]{:S(2)}) copy-start(bf16[256,32,512]{2,1,0:T(8,128)(2,1)} %copy-done.2) | copy-start | bytes 25165828
  164.1 56.6 %collective-permute-start.3 = (bf16[256,16,128]{2,1,0:T(8,128)(2,1)}, bf16[256,16,128]{2,1,0:T(8,128)(2,1)S(1)}, u32[]{:S(2)}, u32[]{:S(2)}) collective-permute-start(bf16[256,16,128]{2,1,0:T(8,128)(2,1)} %get-tuple-element.53), channel_id=1, source_target_pairs={{0,2},{2,0},{1,3},{3,1},{4,6},{6,4},{5,7},{7,5},{8,10},{10,8},{9,1... | collective-permute-start | bytes 3145736 | tf_op jit(solution)/shard_map/ppermute | solution.py:343
  171.3 1.0 copy-start.7
  179.1 3.4 %copy-start.4 = (bf16[256,32,512]{2,1,0:T(8,128)(2,1)S(1)}, bf16[256,32,512]{2,1,0:T(8,128)(2,1)}, u32[]{:S(2)}) copy-start(bf16[256,32,512]{2,1,0:T(8,128)(2,1)} %copy-done.2) | copy-start | bytes 25165828
  186.2 17.6 %collective-permute-start.1 = (bf16[128,16,128]{2,1,0:T(8,128)(2,1)S(1)}, bf16[128,16,128]{2,1,0:T(8,128)(2,1)S(1)}, u32[]{:S(2)}, u32[]{:S(2)}) collective-permute-start(bf16[128,16,128]{2,1,0:T(8,128)(2,1)S(1)} %get-tuple-element.57), channel_id=1, source_target_pairs={{0,2},{2,0},{1,3},{3,1},{4,6},{6,4},{5,7},{7,5},{8,10},{10,8},{9,1... | collective-permute-start | bytes 1572872 | tf_op jit(solution)/shard_map/ppermute | solution.py:343
  187.8 4.3 %copy-start.8 = (bf16[256,16,128]{2,1,0:T(8,128)(2,1)S(1)}, bf16[256,16,128]{2,1,0:T(8,128)(2,1)}, u32[]{:S(2)}) copy-start(bf16[256,16,128]{2,1,0:T(8,128)(2,1)} %copy-done.7) | copy-start | bytes 3145732
  191.5 23.5 %collective-permute-start = (bf16[128,16,128]{2,1,0:T(8,128)(2,1)S(1)}, bf16[128,16,128]{2,1,0:T(8,128)(2,1)S(1)}, u32[]{:S(2)}, u32[]{:S(2)}) collective-permute-start(bf16[128,16,128]{2,1,0:T(8,128)(2,1)S(1)} %get-tuple-element.58), channel_id=1, source_target_pairs={{0,2},{2,0},{1,3},{3,1},{4,6},{6,4},{5,7},{7,5},{8,10},{10,8},{9,1... | collective-permute-start | bytes 1572872 | tf_op jit(solution)/shard_map/ppermute | solution.py:343
  192.1 45.4 %collective-permute-start.4 = (bf16[256,16,128]{2,1,0:T(8,128)(2,1)S(1)}, bf16[256,16,128]{2,1,0:T(8,128)(2,1)S(1)}, u32[]{:S(2)}, u32[]{:S(2)}) collective-permute-start(bf16[256,16,128]{2,1,0:T(8,128)(2,1)S(1)} %copy-done.8), channel_id=1, source_target_pairs={{0,2},{2,0},{1,3},{3,1},{4,6},{6,4},{5,7},{7,5},{8,10},{10,8},{9,1... | collective-permute-start | bytes 3145736 | tf_op jit(solution)/shard_map/ppermute | solution.py:343
  241.3 3.8 %collective-permute-start.5 = (f32[32,96]{1,0:T(8,128)S(1)}, f32[32,96]{1,0:T(8,128)S(1)}, u32[]{:S(2)}, u32[]{:S(2)}) collective-permute-start(f32[32,96]{1,0:T(8,128)S(1)} %maximum_select_fusion.2), channel_id=1, source_target_pairs={{0,2},{2,0},{1,3},{3,1},{4,6},{6,4},{5,7},{7,5},{8,10},{10,8},{9,1... | collective-permute-start | bytes 36872 | tf_op jit(solution)/shard_map/ppermute | solution.py:353
Sparse Core Ops, SparseCore 0:
  9.0 25.8 all-gather.1

commit v3 on v1

v3 whole, which is shorter than its diff:
```python
import jax
import jax.numpy as jnp
from jax import lax
from jax.experimental import pallas as pl
from jax.experimental.pallas import tpu as pltpu
from jax.sharding import PartitionSpec as P

BS = 16
ABLK = 16
CHUNK = 128


def shift(x, axis, by):
    count = lax.axis_size(axis)
    pairs = [(i, i + by) for i in range(count) if 0 <= i + by < count]
    return lax.ppermute(x, axis, pairs)


def spread(blocks, size):
    row = lax.broadcasted_iota(jnp.int32, (blocks, size), 0)
    col = lax.broadcasted_iota(jnp.int32, (blocks, size), 1)
    return (row == col // BS).astype(jnp.bfloat16)


def widen_last(mask, size):
    count = mask.shape[-1]
    flat = mask.astype(jnp.bfloat16).reshape(-1, count)
    wide = jnp.dot(flat, spread(count, size), preferred_element_type=jnp.float32)
    return wide.astype(jnp.bfloat16).reshape(mask.shape[:-1] + (size,))


def mask_green(green, blocks):
    count = blocks.shape[0]
    wide = widen_last(blocks, green.shape[1])
    shaped = green.reshape(count, green.shape[0] // count, green.shape[1])
    return (shaped * wide[:, None, :]).reshape(green.shape)


def mask_three(three, mask):
    wide = widen_last(mask, three.shape[2])
    shaped = three.reshape(mask.shape[0], BS, mask.shape[1], ABLK, three.shape[2])
    return (shaped * wide[:, None, :, None, :]).reshape(three.shape)


PARTS = 4
STEP = 64
MESH = pl.DeviceIdType.MESH


def pair_kernel(
    three_ref, wide_ref, occ_in, virt_in, occ_wide, virt_wide, out_ref,
    held, oth, before, after, green, left, right, send, keep, recv, mine, extra,
    load_sem, green_send, green_recv, pair_send, pair_recv, up_send, up_recv,
    down_send, down_recv, back_send, back_recv, sum_sem,
):
    half, aux, depth = held.shape
    share = aux // 2
    full = 2 * half
    part = half // PARTS
    rows_g = occ_in.shape[0]
    subs = lax.axis_size("sub")
    count = lax.axis_size("blk") * subs
    me = lax.axis_index("blk") * subs + lax.axis_index("sub")
    ao = lax.axis_index("ao")
    pair_id = {"ao": 1 - ao}
    has_above, has_below = me < count - 1, me > 0

    def at_index(index):
        return {"blk": index // subs, "sub": index % subs}

    above_id = at_index(jnp.minimum(me + 1, count - 1))
    below_id = at_index(jnp.maximum(me - 1, 0))
    peers = [at_index(lax.rem(me + d, count)) for d in range(1, count)]
    spans = [pl.ds(k * part, part) for k in range(PARTS)]
    loads = [
        pltpu.make_async_copy(three_ref.at[s], held.at[s], load_sem.at[k])
        for k, s in enumerate(spans)
    ]
    for copy in loads:
        copy.start()
    barrier = pltpu.get_barrier_semaphore()
    for device in [pair_id] + peers:
        pl.semaphore_signal(barrier, inc=1, device_id=device, device_id_type=MESH)

    own_rows = pl.ds(pl.multiple_of(me * rows_g, rows_g), rows_g)
    green[0, own_rows] = occ_in[...]
    green[1, own_rows] = virt_in[...]

    def remote(src, dst, send_sem, recv_sem, device):
        return pltpu.make_async_remote_copy(
            src_ref=src, dst_ref=dst, send_sem=send_sem, recv_sem=recv_sem,
            device_id=device, device_id_type=MESH,
        )

    ours = pl.ds(pl.multiple_of(ao * share, share), share)
    theirs = pl.ds(pl.multiple_of((1 - ao) * share, share), share)
    greens = [
        remote(green.at[g, own_rows], green.at[g, own_rows],
               green_send.at[g, d], green_recv.at[g, d], peers[d])
        for g in (0, 1) for d in range(count - 1)
    ]
    pairs = [
        remote(held.at[s, theirs], oth.at[s], pair_send.at[k], pair_recv.at[k], pair_id)
        for k, s in enumerate(spans)
    ]
    ups = [
        remote(held.at[s], before.at[s], up_send.at[k], up_recv.at[k], above_id)
        for k, s in enumerate(spans)
    ]
    downs = [
        remote(held.at[s], after.at[s], down_send.at[k], down_recv.at[k], below_id)
        for k, s in enumerate(spans)
    ]
    for k in range(PARTS):
        loads[k].wait()

        @pl.loop(0, part // BS)
        def _(i, k=k):
            row = k * (part // BS) + i
            for j in range(aux // ABLK):
                mask = wide_ref[pl.ds(row * (aux // ABLK) + j, 1), :].astype(jnp.bfloat16)
                at = (pl.ds(row * BS, BS), pl.ds(j * ABLK, ABLK))
                held[at] = held[at] * mask[None]

        if k == 0:
            pl.semaphore_wait(barrier, count)
        pairs[k].start()
        if k == 0:
            for copy in greens:
                copy.start()

        @pl.when(has_above)
        def _(k=k):
            ups[k].start()

        @pl.when(has_below)
        def _(k=k):
            downs[k].start()

    @pl.when(jnp.logical_not(has_below))
    def _():
        @pl.loop(0, half)
        def _(i):
            before[i] = jnp.zeros((aux, depth), jnp.bfloat16)

    @pl.when(jnp.logical_not(has_above))
    def _():
        @pl.loop(0, half)
        def _(i):
            after[i] = jnp.zeros((aux, depth), jnp.bfloat16)

    for copy in greens:
        copy.wait()
    for g, wide in ((0, occ_wide), (1, virt_wide)):

        @pl.loop(0, full // BS)
        def _(i, g=g, wide=wide):
            at = pl.ds(i * BS, BS)
            green[g, at] = green[g, at] * wide[pl.ds(i, 1), :].astype(jnp.bfloat16)

    def to_left(source, start, stop, first_n, c):
        lanes = pl.ds(c * CHUNK, CHUNK)

        @pl.loop(start // STEP, stop // STEP)
        def _(i):
            rows = source(i * STEP).reshape(STEP * share, depth)
            at = pl.multiple_of((first_n + i * STEP) * share, STEP * share)
            left[pl.ds(at, STEP * share), :] = jnp.dot(
                rows, green[0, :, lanes], preferred_element_type=jnp.float32
            )

    def of_own(n):
        return held[pl.ds(n, STEP), ours]

    def of_oth(n):
        return oth[pl.ds(n, STEP)]

    def to_right(c):
        for p in range(0, share, 2):
            both = [left[pl.ds(p + k, full, stride=share), :].astype(jnp.bfloat16) for k in (0, 1)]
            out = lax.dot_general(
                green[1],
                jnp.concatenate(both, axis=1),
                (((0,), (0,)), ((), ())),
                preferred_element_type=jnp.float32,
            )
            for k in (0, 1):
                right[pl.ds(p + k, full, stride=share), :] = out[:, k * CHUNK : (k + 1) * CHUNK]

    def out_of_right(ref, c, first_s):
        @pl.loop(0, half // STEP)
        def _(i):
            at = pl.multiple_of((first_s + i * STEP) * share, STEP * share)
            rows = right[pl.ds(at, STEP * share), :].astype(jnp.bfloat16)
            ref[c, pl.ds(i * STEP, STEP)] = rows.reshape(STEP, share, CHUNK)

    def band(ref, c, start, stop):
        lanes = pl.ds(c * CHUNK, CHUNK)

        def some(i, total):
            for k in range(0, 16, 2):
                s = i * 16 + k
                rights = jnp.concatenate([ref[c, s], ref[c, s + 1]], axis=1)
                threes = [
                    jnp.concatenate([t[s, :, lanes], t[s + 1, :, lanes]], axis=1)
                    for t in (before, held, after)
                ]
                total += lax.dot_general(
                    rights, jnp.concatenate(threes, axis=0), (((1,), (1,)), ((), ())),
                    preferred_element_type=jnp.float32,
                )
            return total

        zero = jnp.zeros((share, 3 * aux), jnp.float32)
        return lax.fori_loop(start // 16, stop // 16, some, zero)

    chunks = depth // CHUNK
    cuts = [(c, 0, half) for c in range(chunks - 1)]
    cuts += [(chunks - 1, 0, half // 2), (chunks - 1, half // 2, half)]
    backs = [
        remote(send.at[c, pl.ds(start, stop - start)], recv.at[c, pl.ds(start, stop - start)],
               back_send.at[k], back_recv.at[k], pair_id)
        for k, (c, start, stop) in enumerate(cuts)
    ]
    own_n, oth_n = ao * half, (1 - ao) * half
    for c in range(chunks):
        to_left(of_own, 0, half, own_n, c)
        for k in range(PARTS):
            if c == 0:
                pairs[k].wait()
            to_left(of_oth, k * part, (k + 1) * part, oth_n, c)
        to_right(c)
        out_of_right(send, c, oth_n)
        for k, cut in enumerate(cuts):
            if cut[0] == c:
                backs[k].start()
        out_of_right(keep, c, own_n)

    for k in range(PARTS):

        @pl.when(has_above)
        def _(k=k):
            ups[k].wait_send()
            downs[k].wait_recv()

        @pl.when(has_below)
        def _(k=k):
            downs[k].wait_send()
            ups[k].wait_recv()

    total = band(keep, 0, 0, half)
    for c in range(1, chunks):
        total += band(keep, c, 0, half)
    mine[ours] = total
    total = jnp.zeros((share, 3 * aux), jnp.float32)
    for k, (c, start, stop) in enumerate(cuts):
        backs[k].wait()
        total += band(recv, c, start, stop)
    mine[theirs] = total
    last = remote(mine, extra, sum_sem.at[0], sum_sem.at[1], pair_id)
    last.start()
    last.wait()
    out_ref[...] = mine[...] + extra[...]


def pair_call(three, wide, g_occ, g_virt, occ_wide, virt_wide, peers):
    half, aux, depth = three.shape
    share = aux // 2
    vmem = pl.BlockSpec(memory_space=pltpu.VMEM)
    part = (half, share, depth)
    back = (depth // CHUNK, half, share, CHUNK)
    dma = pltpu.SemaphoreType.DMA
    backs = depth // CHUNK + 1
    return pl.pallas_call(
        pair_kernel,
        out_shape=jax.ShapeDtypeStruct((aux, 3 * aux), jnp.float32),
        in_specs=[pl.BlockSpec(memory_space=pl.ANY)] + [vmem] * 5,
        out_specs=vmem,
        scratch_shapes=[
            pltpu.VMEM(three.shape, three.dtype),
            pltpu.VMEM(part, three.dtype),
            pltpu.VMEM(three.shape, three.dtype),
            pltpu.VMEM(three.shape, three.dtype),
            pltpu.VMEM((2, depth, depth), three.dtype),
            pltpu.VMEM((2 * half * share, CHUNK), jnp.float32),
            pltpu.VMEM((2 * half * share, CHUNK), jnp.float32),
            pltpu.VMEM(back, three.dtype),
            pltpu.VMEM(back, three.dtype),
            pltpu.VMEM(back, three.dtype),
            pltpu.VMEM((aux, 3 * aux), jnp.float32),
            pltpu.VMEM((aux, 3 * aux), jnp.float32),
            dma((PARTS,)),
            dma((2, peers)),
            dma((2, peers)),
        ]
        + [dma((PARTS,))] * 6
        + [dma((backs,))] * 2
        + [dma((2,))],
        compiler_params=pltpu.CompilerParams(
            collective_id=0, has_side_effects=True, vmem_limit_bytes=58 * 1024 * 1024
        ),
        cost_estimate=pl.CostEstimate(
            flops=10**11, bytes_accessed=2 * half * aux * depth, transcendentals=0
        ),
        name="pair",
    )(three, wide, g_occ, g_virt, occ_wide, virt_wide)


def body_pair(three, three_mask, g_occ, g_virt, occ_mask, virt_mask):
    half, aux, depth = three.shape
    masks = jnp.concatenate([three_mask.reshape(-1, depth // BS), occ_mask, virt_mask], axis=0)
    wide = widen_last(masks, depth).astype(jnp.float32)
    count = three_mask.shape[0] * three_mask.shape[1]
    blocks = occ_mask.shape[0]
    peers = lax.axis_size(("blk", "sub")) - 1
    chi = pair_call(
        three, wide[:count], g_occ, g_virt,
        wide[count : count + blocks], wide[count + blocks :], peers,
    )
    return chi.reshape(aux, 3, aux)


def body_any(three, three_mask, g_occ, g_virt, occ_mask, virt_mask):
    eff = mask_three(three, three_mask)
    occ = mask_green(lax.all_gather(g_occ, ("blk", "sub"), axis=0, tiled=True), occ_mask)
    virt = mask_green(lax.all_gather(g_virt, ("blk", "sub"), axis=0, tiled=True), virt_mask)
    whole = lax.all_to_all(eff, "ao", split_axis=1, concat_axis=0, tiled=True)
    left = lax.dot_general(
        whole, occ, (((2,), (0,)), ((), ())), preferred_element_type=jnp.float32
    ).astype(jnp.bfloat16)
    right = lax.dot_general(
        virt, left, (((0,), (0,)), ((), ())), preferred_element_type=jnp.float32
    ).astype(jnp.bfloat16)
    right = lax.all_to_all(right, "ao", split_axis=0, concat_axis=1, tiled=True)
    tiles = [
        lax.dot_general(
            right, other, (((0, 2), (0, 2)), ((), ())), preferred_element_type=jnp.float32
        )
        for other in (shift(eff, ("blk", "sub"), 1), eff, shift(eff, ("blk", "sub"), -1))
    ]
    return lax.psum(jnp.stack(tiles, axis=1), "ao")


def solution(mesh):
    placed = (
        P(("parts", "ao"), ("blk", "sub"), None),
        P(("parts", "ao"), ("blk", "sub"), None),
        P(("parts", "blk", "sub"), None),
        P(("parts", "blk", "sub"), None),
        P("parts", None),
        P("parts", None),
    )
    return jax.shard_map(
        body_pair if mesh.shape["ao"] == 2 else body_any,
        mesh=mesh,
        in_specs=placed,
        out_specs=P(("parts", "blk", "sub"), None, None),
        check_vma=False,
    )
```

time: 258 us -> 205 us (0.79)
  waiting for transfers between devices: 112 us -> 0 us
  Pallas kernels: 90.4 us -> 197 us
  between operations: 13.6 us -> 0.04 us
  other arithmetic: 14.2 us -> 0.75 us
  starting transfers between devices: 10.1 us -> 0 us
  blocking collectives: 8.85 us -> 0 us
    pallas_call x12 -> x1, Pallas kernels: 90.4 us -> 197 us  [pair_call(): pl.pallas_call(pair_kernel, out_shape=jax.ShapeDtypeStruct((aux, 3 * aux)...]
    ppermute x7 -> x0, waiting for transfers between devices: 84 us -> none  [the longest x1 60.1 us: body_pair(): oth = lax.ppermute(jnp.where(first, high, low), 'ao', swap)]
    all_gather x1 -> x0, waiting for transfers between devices: 28.1 us -> none  [body_pair(): lax.all_gather(jnp.stack([g_occ, g_virt]), ('blk', 'sub'), axis=1, tiled=...]
    ppermute x7 -> x0, starting transfers between devices: 10.1 us -> none  [the longest x4 4.33 us: body_pair(): recv = lax.ppermute(send, 'ao', swap)]
    psum x1 -> x0, blocking collectives: 8.85 us -> none  [body_pair(): return lax.psum(chi, 'ao').reshape(aux, 3, aux)]
    select_n x4 -> x0, other arithmetic: 7.4 us -> none  [the longest x1 5.78 us: body_pair(): oth = lax.ppermute(jnp.where(first, high, low), 'ao', swap)]
    mul x2 -> x0, other arithmetic: 5.33 us -> none  [the longest x1 5.28 us: mask_three(): return (shaped * wide[:, None, :, None, :]).reshape(three.shape)]
  transfers between devices with their start and end apart: 8 -> 0, of which waited for: 4 -> 0; matrix products, arithmetic and copies ran while one was open for 4% -> 0% of each run, Pallas kernels for 33% -> 0%
where the time goes in v3:
time: 205 us; the launch traced here: 202 us
  Pallas kernels  197 us (96%)
  local copies, waits for them, and re-layouts  3.78 us (2%)
    pallas_call x1, Pallas kernels, pair_call(): pl.pallas_call(pair_kernel, out_shape=jax.ShapeDtypeStruct((aux, 3 * aux)...  197 us

profile of v3, /device:TPU:8, one launch (start us, length us, event | category | flops | bytes accessed | tf_op | source)
XLA Modules:
  0.0 201.7 jit_solution(438349323493700967)
XLA Ops:
  0.0 0.7 convert.10
  0.7 0.1 copy.15
  0.8 0.8 copy.13
  1.6 0.8 copy.14
  2.4 0.3 fusion
  2.7 0.7 fusion.13
  3.4 196.8 %pair.1 = f32[32,96]{1,0:T(8,128)} custom-call(bf16[256,32,512]{2,1,0:T(8,128)(2,1)} %three_ref.1, f32[32,512]{1,0:T(8,128)} %get-tuple-element.7.wide_ref, bf16[64,512]{1,0:T(8,128)(2,1)} %occ_in.1, bf16[64,512]{1,0:T(8,128)(2,1)} %virt_in.1, f32[32,512]{1,0:T(8,128)} %get-tuple-element.6.occ_wide, f32[32,512]{1,0:T(8,128)} %get-tuple-element.5.virt_wide), custom_call_target="tpu_custom_call" | custom-call | flops 99999997952 | bytes 8388608 | tf_op jit(solution)/shard_map/pair/pallas_call | solution.py:274
  200.2 0.8 reshape.8
  201.0 0.6 copy.16
  (4 shorter events, 0.0 us)

commit v4 on v3

--- a/solution.py
+++ b/solution.py
@@ -48,8 +48,9 @@
 
 
 def pair_kernel(
-    three_ref, wide_ref, occ_in, virt_in, occ_wide, virt_wide, out_ref,
+    three_ref, mask_ref, occ_in, virt_in, occ_mask, virt_mask, out_ref,
     held, oth, before, after, green, left, right, send, keep, recv, mine, extra,
+    wide_ref, occ_wide, virt_wide,
     load_sem, green_send, green_recv, pair_send, pair_recv, up_send, up_recv,
     down_send, down_recv, back_send, back_recv, sum_sem,
 ):
@@ -82,6 +83,12 @@
     for device in [pair_id] + peers:
         pl.semaphore_signal(barrier, inc=1, device_id=device, device_id_type=MESH)
 
+    def widen(mask):
+        spreading = spread(mask.shape[1], depth)
+        flat = mask.astype(jnp.float32).astype(jnp.bfloat16)
+        return jnp.dot(flat, spreading, preferred_element_type=jnp.float32)
+
+    wide_ref[...] = widen(mask_ref[...])
     own_rows = pl.ds(pl.multiple_of(me * rows_g, rows_g), rows_g)
     green[0, own_rows] = occ_in[...]
     green[1, own_rows] = virt_in[...]
@@ -151,6 +158,8 @@
 
     for copy in greens:
         copy.wait()
+    occ_wide[...] = widen(occ_mask[...])
+    virt_wide[...] = widen(virt_mask[...])
     for g, wide in ((0, occ_wide), (1, virt_wide)):
 
         @pl.loop(0, full // BS)
@@ -175,17 +184,20 @@
     def of_oth(n):
         return oth[pl.ds(n, STEP)]
 
-    def to_right(c):
+    def to_right(first_n, have, add):
         for p in range(0, share, 2):
-            both = [left[pl.ds(p + k, full, stride=share), :].astype(jnp.bfloat16) for k in (0, 1)]
+            both = [left[pl.ds(first_n * share + p + k, have, stride=share), :] for k in (0, 1)]
+            both = [x.astype(jnp.bfloat16) for x in both]
             out = lax.dot_general(
-                green[1],
+                green[1, pl.ds(first_n, have)],
                 jnp.concatenate(both, axis=1),
                 (((0,), (0,)), ((), ())),
                 preferred_element_type=jnp.float32,
             )
             for k in (0, 1):
-                right[pl.ds(p + k, full, stride=share), :] = out[:, k * CHUNK : (k + 1) * CHUNK]
+                rows = pl.ds(p + k, full, stride=share)
+                term = out[:, k * CHUNK : (k + 1) * CHUNK]
+                right[rows, :] = right[rows, :] + term if add else term
 
     def out_of_right(ref, c, first_s):
         @pl.loop(0, half // STEP)
@@ -222,14 +234,20 @@
                back_send.at[k], back_recv.at[k], pair_id)
         for k, (c, start, stop) in enumerate(cuts)
     ]
-    own_n, oth_n = ao * half, (1 - ao) * half
+    own_n = pl.multiple_of(ao * half, half)
+    oth_n = pl.multiple_of((1 - ao) * half, half)
     for c in range(chunks):
         to_left(of_own, 0, half, own_n, c)
+        if c == 0:
+            to_right(own_n, half, False)
         for k in range(PARTS):
             if c == 0:
                 pairs[k].wait()
             to_left(of_oth, k * part, (k + 1) * part, oth_n, c)
-        to_right(c)
+        if c == 0:
+            to_right(oth_n, half, True)
+        else:
+            to_right(0, full, False)
         out_of_right(send, c, oth_n)
         for k, cut in enumerate(cuts):
             if cut[0] == c:
@@ -263,7 +281,7 @@
     out_ref[...] = mine[...] + extra[...]
 
 
-def pair_call(three, wide, g_occ, g_virt, occ_wide, virt_wide, peers):
+def pair_call(three, mask, g_occ, g_virt, occ_mask, virt_mask, peers):
     half, aux, depth = three.shape
     share = aux // 2
     vmem = pl.BlockSpec(memory_space=pltpu.VMEM)
@@ -289,6 +307,9 @@
             pltpu.VMEM(back, three.dtype),
             pltpu.VMEM((aux, 3 * aux), jnp.float32),
             pltpu.VMEM((aux, 3 * aux), jnp.float32),
+            pltpu.VMEM((mask.shape[0], depth), jnp.float32),
+            pltpu.VMEM((occ_mask.shape[0], depth), jnp.float32),
+            pltpu.VMEM((virt_mask.shape[0], depth), jnp.float32),
             dma((PARTS,)),
             dma((2, peers)),
             dma((2, peers)),
@@ -303,20 +324,14 @@
             flops=10**11, bytes_accessed=2 * half * aux * depth, transcendentals=0
         ),
         name="pair",
-    )(three, wide, g_occ, g_virt, occ_wide, virt_wide)
+    )(three, mask, g_occ, g_virt, occ_mask, virt_mask)
 
 
 def body_pair(three, three_mask, g_occ, g_virt, occ_mask, virt_mask):
     half, aux, depth = three.shape
-    masks = jnp.concatenate([three_mask.reshape(-1, depth // BS), occ_mask, virt_mask], axis=0)
-    wide = widen_last(masks, depth).astype(jnp.float32)
-    count = three_mask.shape[0] * three_mask.shape[1]
-    blocks = occ_mask.shape[0]
     peers = lax.axis_size(("blk", "sub")) - 1
-    chi = pair_call(
-        three, wide[:count], g_occ, g_virt,
-        wide[count : count + blocks], wide[count + blocks :], peers,
-    )
+    mask = three_mask.reshape(-1, depth // BS)
+    chi = pair_call(three, mask, g_occ, g_virt, occ_mask, virt_mask, peers)
     return chi.reshape(aux, 3, aux)
 
 

time: 205 us -> 201 us (0.980)
  local copies, waits for them, and re-layouts: 3.78 us -> 1.43 us
where the time goes in v4:
time: 201 us; the launch traced here: 198 us
  Pallas kernels  197 us (98%)
    pallas_call x1, Pallas kernels, pair_call(): pl.pallas_call(pair_kernel, out_shape=jax.ShapeDtypeStruct((aux, 3 * aux)...  197 us

profile of v4, /device:TPU:8, one launch (start us, length us, event | category | flops | bytes accessed | tf_op | source)
XLA Modules:
  0.0 198.0 jit_solution(7922607893177643861)
XLA Ops:
  0.0 196.6 %pair.1 = f32[32,96]{1,0:T(8,128)} custom-call(bf16[256,32,512]{2,1,0:T(8,128)(2,1)} %three_ref.1, s32[32,32]{1,0:T(8,128)} %bitcast.1, bf16[64,512]{1,0:T(8,128)(2,1)} %occ_in.1, bf16[64,512]{1,0:T(8,128)(2,1)} %virt_in.1, s32[32,32]{1,0:T(8,128)} %occ_mask.1, s32[32,32]{1,0:T(8,128)} %virt_mask.1), custom_call_target="tpu_custom_call" | custom-call | flops 99999997952 | bytes 8388608 | tf_op jit(solution)/shard_map/pair/pallas_call | solution.py:292
  196.6 0.8 reshape.7
  197.4 0.6 copy.8
